TPU v7x, 32 devices: a whole 2x2x4 slice. The times are simulated.
32 devices in a mesh: slab: 32 (over z, y, x, core), gy: 1.
Axes of the slice: x: 2, y: 2, z: 4, core: 2. Of those that a mesh axis runs over, the one named last changes fastest.
Arguments:
- electrostatic_voltages: float32 [256, 64, 1024], P('slab', 'gy'), may hold values from -6 to 6
- initial_electrons: float32 [256, 64, 1024], P('slab', 'gy'), may hold values from 0.5 to 2
- creation_amounts: float32 [256, 64, 1024], P('slab', 'gy'), may hold values from 0.2 to 5
- annihilation_coefficient: float32 [256, 64, 1024], P('slab', 'gy'), may hold values from 0.5 to 2
- crystal_orientation_class: int32 [256, 64, 1024], P('slab', 'gy'), may hold values from 0 to 3
- crystal_barrier_shift: float32 [4], replicated, may hold values from -1.5 to 1.5
- restrict_matrix_first: float32 [128, 256], replicated, may hold values from 0 to 1, as said below
- restrict_matrix_second: float32 [32, 64], P('gy'), may hold values from 0 to 1, as said below
- restrict_matrix_third: float32 [256, 1024], replicated, may hold values from 0 to 1, as said below
- cooling_coefficient: float32 [256, 32, 128], P('slab', 'gy'), may hold values from 0.05 to 1
- initial_warming: float32 [256, 32, 128], P('slab', 'gy'), may hold values from 0.5 to 1.5
Outputs:
- density_out: float32 [256, 64, 1024], P('slab', 'gy')
- thermal_out: float32 [256, 32, 128], P('slab', 'gy')
- fine_mesh_warming: float32 [256, 64, 1024], P('slab', 'gy')
Inputs may be any that keep to these rules, and one draw needn't show every extreme that they name: `restrict_matrix_first`: row a is nonnegative, nonzero at most on columns 2a - 1 to 2a + 2, and sums to 1. `restrict_matrix_second`: row b, with t = b % 32, is nonnegative, nonzero at most on columns 2t - 1 to 2t + 2, and sums to 1. `restrict_matrix_third`: row c is nonnegative, nonzero at most on columns 4c - 2 to 4c + 5, and sums to 1.
All inputs are finite; a program needn't handle non-finite values.
Results may differ from a plain program's by a relative error of at most 0.0003.
Values sent between devices are 32-bit elements; how exact they have to be, the bound alone decides.
A program may use at most 64 MiB of HBM per device.

v0:
```python
import functools

import jax
import jax.numpy as jnp
from jax import lax
from jax.experimental import pallas as pl
from jax.experimental.pallas import tpu as pltpu
from jax.sharding import PartitionSpec as P

MESH = pl.DeviceIdType.MESH
HIGHEST = lax.Precision.HIGHEST
GRAINS = 4
HEAT_SWEEPS = 3
PAD = 8
MIB = 1024 * 1024


def bernoulli(u):
    small = jnp.abs(u) < 0.03125
    series = 1.0 + u * (u * (1.0 / 12.0) - 0.5)
    return jnp.where(small, series, u / (jnp.exp(u) - 1.0))


def device_kernel(
    slabs, yblocks,
    shift_ref, wx_ref, volt_hbm, start_hbm, gen_hbm, ann_hbm, grain_hbm, r3t_hbm, ky_ref,
    dens_hbm, src_ref,
    E, N0, N1, N2, GEN, ANN, GR, RD, BX, MX, BY, MY, BZ, MZ, B0, U0, HEAT, R3T, HZ, SEND, GOTL, GOTR,
    in_sem, out_sem, send_sem, recv_sem,
):
    X, Y, Z = GEN.shape
    me = lax.axis_index("slab")
    gy = lax.axis_index("gy")
    rows = slice(PAD, PAD + Y)
    chunks = range(0, Y, 8)
    t_rows = src_ref.shape[1]

    loads = {}

    def load(key, src, dst):
        copy = pltpu.make_async_copy(src, dst, in_sem.at[len(loads)])
        copy.start()
        loads[key] = copy

    inner = pl.ds(1, X - 2)
    for layer in (0, X - 1):
        load(("v", layer), volt_hbm.at[layer], E.at[layer + 1, pl.ds(PAD, Y)])
        load(("g", layer), grain_hbm.at[layer], GR.at[layer])
        load(("n", layer), start_hbm.at[layer], N0.at[layer + 1, pl.ds(PAD, Y)])
    load("v", volt_hbm.at[inner], E.at[pl.ds(2, X - 2), pl.ds(PAD, Y)])
    load("g", grain_hbm.at[inner], GR.at[inner])
    load("a", ann_hbm, ANN)
    load("n", start_hbm.at[inner], N0.at[pl.ds(2, X - 2), pl.ds(PAD, Y)])
    load("gen", gen_hbm, GEN)
    load("r3t", r3t_hbm, R3T)

    zero_rows = jnp.zeros((X + 2, PAD, Z), jnp.float32)
    zero_layer = jnp.zeros((Y, Z), jnp.float32)
    for buf in (E, N0, N1, N2):
        buf[:, 0:PAD, :] = zero_rows
        buf[:, PAD + Y:2 * PAD + Y, :] = zero_rows

        @pl.when(me == 0)
        def _():
            buf[0, rows, :] = zero_layer

        @pl.when(me == slabs - 1)
        def _():
            buf[X + 1, rows, :] = zero_layer

    @pl.when(me == 0)
    def _():
        GOTL[...] = jnp.zeros_like(GOTL)

    @pl.when(me == slabs - 1)
    def _():
        GOTR[...] = jnp.zeros_like(GOTR)

    x_sides = [(me > 0, (me - 1, gy)), (me < slabs - 1, (me + 1, gy))]
    y_sides = [] if yblocks == 1 else [(gy > 0, (me, gy - 1)), (gy < yblocks - 1, (me, gy + 1))]

    barrier = pltpu.get_barrier_semaphore()
    for has, device in x_sides + y_sides:
        @pl.when(has)
        def _():
            pl.semaphore_signal(barrier, inc=1, device_id=device, device_id_type=MESH)
    peers = sum(has.astype(jnp.int32) for has, _ in x_sides + y_sides)
    pl.semaphore_wait(barrier, peers)

    def side_copy(slot, d, device, src, dst):
        return pltpu.make_async_remote_copy(
            src_ref=src, dst_ref=dst, send_sem=send_sem.at[slot, d], recv_sem=recv_sem.at[slot, d],
            device_id=device, device_id_type=MESH,
        )

    def x_copies(slot, buf):
        body = pl.ds(PAD, Y)
        return [
            (has, side_copy(slot, d, device, buf.at[1 if d == 0 else X, body], buf.at[X + 1 if d == 0 else 0, body]))
            for d, (has, device) in enumerate(x_sides)
        ]

    def y_copies(slot, buf):
        layers = pl.ds(1, X)
        return [
            (has, side_copy(
                slot, 2 + d, device,
                buf.at[layers, pl.ds(PAD if d == 0 else Y, PAD)],
                buf.at[layers, pl.ds(PAD + Y if d == 0 else 0, PAD)],
            ))
            for d, (has, device) in enumerate(y_sides)
        ]

    def start(copies):
        for has, copy in copies:
            @pl.when(has)
            def _():
                copy.start()

    def finish(copies):
        for (has, copy), (_, mirror) in zip(copies, copies[::-1]):
            @pl.when(has)
            def _():
                copy.wait_send()
                mirror.wait_recv()

    def exchange_y(slot, buf):
        copies = y_copies(slot, buf)
        start(copies)
        finish(copies)

    def over_layers(first, last, body):
        def step(x, carry):
            body(x)
            return carry
        lax.fori_loop(first, last, step, 0)

    shifts = [shift_ref[g] for g in range(GRAINS)]

    def effective(x):
        for y in chunks:
            grain = GR[x, y:y + 8, :]
            shift = jnp.where(grain == 0, shifts[0], 0.0)
            for g in range(1, GRAINS):
                shift = jnp.where(grain == g, shifts[g], shift)
            E[x + 1, PAD + y:PAD + y + 8, :] = E[x + 1, PAD + y:PAD + y + 8, :] + shift

    for layer in (0, X - 1):
        loads[("v", layer)].wait()
        loads[("g", layer)].wait()
        effective(layer)
    e_copies = x_copies(0, E)
    start(e_copies)
    for layer in (0, X - 1):
        loads[("n", layer)].wait()
    n_copies = x_copies(1, N0)
    start(n_copies)
    loads["v"].wait()
    loads["g"].wait()
    over_layers(1, X - 1, effective)
    loads["n"].wait()
    if y_sides:
        exchange_y(0, E)
        exchange_y(1, N0)
    loads["a"].wait()

    lane = lax.broadcasted_iota(jnp.int32, (8, Z), 1)
    first_lane = lane == 0
    last_lane = lane == Z - 1
    lane0 = lax.broadcasted_iota(jnp.int32, (8, 128), 1) == 0

    def up_z(v):
        return jnp.where(last_lane, 0.0, pltpu.roll(v, Z - 1, 1))

    def down_z(v):
        return jnp.where(first_lane, 0.0, pltpu.roll(v, 1, 1))

    def yz_faces(x):
        u = E[x + 1, PAD:PAD + 8, :] - E[x + 1, PAD - 1:PAD + 7, :]
        b = bernoulli(u)
        BY[x, PAD - 1:PAD, :] = b[0:1]
        MY[x, PAD - 1:PAD, :] = b[0:1] + u[0:1]
        for y in chunks:
            r = PAD + y
            e = E[x + 1, r:r + 8, :]
            uy = E[x + 1, r + 1:r + 9, :] - e
            by = bernoulli(uy)
            my = by + uy
            BY[x, r:r + 8, :] = by
            MY[x, r:r + 8, :] = my
            uz = up_z(e) - e
            bz = bernoulli(uz)
            mz = bz + uz
            BZ[x, y:y + 8, :] = bz
            MZ[x, y:y + 8, :] = mz
            e0 = e[:, 0:128]
            b0 = bernoulli(e0)
            B0[x, y:y + 8, :] = jnp.where(lane0, b0, 0.0)
            U0[x, y:y + 8, :] = jnp.where(lane0, 0.5 * e0 * b0, 0.0)
            RD[x, y:y + 8, :] = ANN[x, y:y + 8, :] + my + mz + down_z(bz) + BY[x, r - 1:r + 7, :]
            RD[x, y:y + 8, 0:128] = RD[x, y:y + 8, 0:128] + B0[x, y:y + 8, :]

    over_layers(0, X, yz_faces)

    def x_face(f):
        for y in chunks:
            r = PAD + y
            u = E[f + 1, r:r + 8, :] - E[f, r:r + 8, :]
            b = bernoulli(u)
            BX[f, y:y + 8, :] = b
            MX[f, y:y + 8, :] = b + u

    over_layers(1, X, x_face)
    finish(e_copies)
    x_face(0)
    x_face(X)
    loads["gen"].wait()
    finish(n_copies)

    def sweep(src, dst, first):
        def layer(x):
            for y in chunks:
                r = PAD + y
                c = slice(y, y + 8)
                n = src[x + 1, r:r + 8, :]
                total = GEN[x, c, :] + BX[x + 1, c, :] * src[x + 2, r:r + 8, :] + MX[x, c, :] * src[x, r:r + 8, :]
                total = total + BY[x, r:r + 8, :] * src[x + 1, r + 1:r + 9, :]
                total = total + MY[x, r - 1:r + 7, :] * src[x + 1, r - 1:r + 7, :]
                total = total + BZ[x, c, :] * up_z(n) + down_z(MZ[x, c, :] * n)
                if first:
                    rd = 1.0 / (RD[x, c, :] + MX[x + 1, c, :] + BX[x, c, :])
                    RD[x, c, :] = rd
                else:
                    rd = RD[x, c, :]
                dst[x + 1, r:r + 8, :] = total * rd
        return layer

    first = sweep(N0, N1, True)
    over_layers(0, 1, first)
    over_layers(X - 1, X, first)
    one_copies = x_copies(2, N1)
    start(one_copies)
    over_layers(1, X - 1, first)
    if y_sides:
        exchange_y(2, N1)
    second = sweep(N1, N2, False)
    over_layers(1, X - 1, second)
    finish(one_copies)
    over_layers(0, 1, second)
    over_layers(X - 1, X, second)
    two_copies = x_copies(3, N2)
    start(two_copies)
    out = pltpu.make_async_copy(N2.at[pl.ds(1, X), pl.ds(PAD, Y)], dens_hbm, out_sem)
    out.start()
    if y_sides:
        exchange_y(3, N2)

    def heat(x):
        for y in chunks:
            r = PAD + y
            c = slice(y, y + 8)
            n = N2[x + 1, r:r + 8, :]

            def term(b, m, low, high):
                return (m - b) * (b * high - m * low)

            total = term(BX[x + 1, c, :], MX[x + 1, c, :], n, N2[x + 2, r:r + 8, :])
            total = total + term(BX[x, c, :], MX[x, c, :], N2[x, r:r + 8, :], n)
            total = total + term(BY[x, r:r + 8, :], MY[x, r:r + 8, :], n, N2[x + 1, r + 1:r + 9, :])
            total = total + term(
                BY[x, r - 1:r + 7, :], MY[x, r - 1:r + 7, :], N2[x + 1, r - 1:r + 7, :], n
            )
            fz = term(BZ[x, c, :], MZ[x, c, :], n, up_z(n))
            total = total + fz + down_z(fz)
            HEAT[x, c, :] = 0.5 * total
            HEAT[x, c, 0:128] = HEAT[x, c, 0:128] + U0[x, c, :] * n[:, 0:128]

    over_layers(1, X - 1, heat)
    finish(two_copies)
    over_layers(0, 1, heat)
    over_layers(X - 1, X, heat)

    loads["r3t"].wait()
    HZ[...] = jnp.dot(
        HEAT[...].reshape(X * Y, Z), R3T[...], precision=HIGHEST, preferred_element_type=jnp.float32
    ).reshape(HZ.shape)
    A = X // 2
    parts = []
    for a in range(A + 2):
        total = None
        for x in range(max(0, 2 * a - 3), min(X, 2 * a + 1)):
            piece = wx_ref[a, x] * HZ[x]
            total = piece if total is None else total + piece
        parts.append(total)
    share = jnp.dot(
        ky_ref[...], jnp.concatenate(parts, axis=0), precision=HIGHEST, preferred_element_type=jnp.float32
    )
    SEND[...] = share.reshape(SEND.shape)
    has_l, left = x_sides[0]
    has_r, right = x_sides[1]
    copies = [
        (has_l, side_copy(4, 0, left, SEND.at[pl.ds(0, A)], GOTR)),
        (has_r, side_copy(4, 1, right, SEND.at[pl.ds(2, A)], GOTL)),
    ]
    start(copies)
    finish(copies)
    src_ref[0:A - 2] = GOTL[0:A - 2]
    src_ref[A - 2] = GOTL[A - 2] + SEND[0]
    src_ref[A - 1] = GOTL[A - 1] + SEND[1]
    src_ref[A:2 * A - 2] = SEND[2:A]
    src_ref[2 * A - 2] = SEND[A] + GOTR[0]
    src_ref[2 * A - 1] = SEND[A + 1] + GOTR[1]
    src_ref[2 * A:] = GOTR[2:]
    out.wait()


def thermal_kernel(src_ref, start_ref, rc_ref, out_ref, ta, tb):
    A = out_ref.shape[0] - 2
    T, C = out_ref.shape[1:]
    row = lax.broadcasted_iota(jnp.int32, (T, C), 0)
    col = lax.broadcasted_iota(jnp.int32, (T, C), 1)
    bufs = [start_ref, ta, tb, None]
    width = start_ref.shape[0]
    for sweep in range(HEAT_SWEEPS):
        old = bufs[sweep]
        for a in range(sweep + 1, width - 1 - sweep):
            v = old[a]
            total = src_ref[a - 1] + old[a - 1] + old[a + 1]
            total = total + jnp.where(row == T - 1, 0.0, pltpu.roll(v, T - 1, 0))
            total = total + jnp.where(row == 0, 0.0, pltpu.roll(v, 1, 0))
            total = total + jnp.where(col == C - 1, 0.0, pltpu.roll(v, C - 1, 1))
            total = total + jnp.where(col == 0, 0.0, pltpu.roll(v, 1, 1))
            new = total * rc_ref[a]
            if sweep == HEAT_SWEEPS - 1:
                out_ref[a - HEAT_SWEEPS] = new
            else:
                bufs[sweep + 1][a] = new


def prolong_kernel(wx_ref, t_ref, ky_ref, r3_ref, out_ref, spread):
    X = wx_ref.shape[1]
    A = X // 2
    T, C = t_ref.shape[1:]

    @pl.when(pl.program_id(0) == 0)
    def _():
        for x in range(X):
            total = None
            for a in range(A + 2):
                if max(0, 2 * a - 3) <= x < 2 * a + 1:
                    piece = wx_ref[a, x] * t_ref[a]
                    total = piece if total is None else total + piece
            spread[x * T:(x + 1) * T, :] = total

    part = jnp.dot(ky_ref[...], spread[...], precision=HIGHEST, preferred_element_type=jnp.float32)
    out_ref[...] = jnp.dot(part, r3_ref[...], precision=HIGHEST, preferred_element_type=jnp.float32)


def per_device(
    volt, start, gen, ann, grain, barrier_shift, r1, r2, r3, cooling, warming,
):
    slabs, yblocks = lax.axis_size("slab"), lax.axis_size("gy")
    X, Y, Z = volt.shape
    C, T = r3.shape[0], r2.shape[0]
    CL, _, AT = warming.shape
    A = X // 2
    me = lax.axis_index("slab")
    f32 = jnp.float32

    wx = lax.dynamic_slice(jnp.pad(r1, ((1, 1), (0, 0))), (me * A, me * X), (A + 2, X))
    eye = jnp.eye(X, dtype=f32)
    ky = jnp.einsum("ij,tc->itjc", eye, r2, precision=HIGHEST).reshape(X * T, X * Y)

    both = jnp.stack([warming, 1.0 / (6.0 + cooling)]).reshape(2, CL * T, AT)
    both = jnp.pad(both.transpose(0, 2, 1), ((0, 0), (A, A), (0, 0))).reshape(2, slabs + 2, A, CL * T)
    both = jnp.concatenate([both[:, i:i + slabs] for i in range(3)], axis=2)
    both = both.transpose(1, 0, 2, 3).reshape(slabs, 6 * A, CL * T)
    both = lax.all_to_all(both, "slab", 0, 0, tiled=True)
    both = both.reshape(slabs, 6 * A, CL, T).transpose(1, 3, 0, 2).reshape(2, 3 * A, T, C)

    smem = pl.BlockSpec(memory_space=pltpu.SMEM)
    vmem = pl.BlockSpec(memory_space=pltpu.VMEM)
    anyspace = pl.BlockSpec(memory_space=pl.ANY)
    padded = pltpu.VMEM((X + 2, Y + 2 * PAD, Z), f32)
    block = pltpu.VMEM((X, Y, Z), f32)
    xface = pltpu.VMEM((X + 1, Y, Z), f32)
    yface = pltpu.VMEM((X, Y + PAD, Z), f32)
    edge = pltpu.VMEM((X, Y, 128), f32)
    cells = X * Y * Z
    density, source = pl.pallas_call(
        functools.partial(device_kernel, slabs, yblocks),
        out_shape=(
            jax.ShapeDtypeStruct((X, Y, Z), f32),
            jax.ShapeDtypeStruct((3 * A - 2, T, C), f32),
        ),
        in_specs=[smem, smem] + [anyspace] * 6 + [vmem],
        out_specs=(anyspace, vmem),
        scratch_shapes=[
            padded, padded, padded, padded, block, block, pltpu.VMEM((X, Y, Z), jnp.int32), block,
            xface, xface, yface, yface, block, block, edge, edge, block,
            pltpu.VMEM((Z, C), f32), pltpu.VMEM((X, Y, C), f32), pltpu.VMEM((A + 2, T, C), f32),
            pltpu.VMEM((A, T, C), f32), pltpu.VMEM((A, T, C), f32),
            pltpu.SemaphoreType.DMA((16,)), pltpu.SemaphoreType.DMA,
            pltpu.SemaphoreType.DMA((5, 4)), pltpu.SemaphoreType.DMA((5, 4)),
        ],
        compiler_params=pltpu.CompilerParams(
            collective_id=0, has_side_effects=True, vmem_limit_bytes=58 * MIB
        ),
        cost_estimate=pl.CostEstimate(flops=200 * cells, bytes_accessed=24 * cells, transcendentals=3 * cells),
    )(barrier_shift, wx, volt, start, gen, ann, grain, r3.T, ky[:(A + 2) * T, :(A + 2) * Y])

    if yblocks == 1:
        thermal = pl.pallas_call(
            thermal_kernel,
            out_shape=jax.ShapeDtypeStruct((A + 2, T, C), f32),
            in_specs=[vmem] * 3,
            out_specs=vmem,
            scratch_shapes=[pltpu.VMEM((3 * A, T, C), f32)] * 2,
        )(source, both[0], both[1])
    else:
        thermal = both[0]
        up = [(i, i + 1) for i in range(yblocks - 1)]
        down = [(i + 1, i) for i in range(yblocks - 1)]
        for sweep in range(HEAT_SWEEPS):
            low = lax.ppermute(thermal[:, -1:], "gy", up)
            high = lax.ppermute(thermal[:, :1], "gy", down)
            tall = jnp.concatenate([low, thermal, high], axis=1)
            wide = jnp.pad(thermal, ((0, 0), (0, 0), (1, 1)))
            total = source[sweep:3 * A - 2 - sweep] + thermal[2:] + thermal[:-2]
            total = total + (tall[:, 2:] + tall[:, :-2] + wide[:, :, 2:] + wide[:, :, :-2])[1:-1]
            thermal = total * both[1][sweep + 1:3 * A - 1 - sweep]

    mine = thermal[1:A + 1].reshape(A, T, slabs, CL).transpose(2, 0, 3, 1).reshape(slabs, A, CL * T)
    mine = lax.all_to_all(mine, "slab", 0, 0, tiled=True).reshape(AT, CL * T)
    thermal_out = mine.T.reshape(CL, T, AT)

    steps = 4
    fine = pl.pallas_call(
        prolong_kernel,
        grid=(steps,),
        out_shape=jax.ShapeDtypeStruct((X * Y, Z), f32),
        in_specs=[
            smem, vmem,
            pl.BlockSpec((X * Y // steps, X * T), lambda i: (i, 0)),
            vmem,
        ],
        out_specs=pl.BlockSpec((X * Y // steps, Z), lambda i: (i, 0)),
        scratch_shapes=[pltpu.VMEM((X * T, C), f32)],
        compiler_params=pltpu.CompilerParams(vmem_limit_bytes=24 * MIB),
        cost_estimate=pl.CostEstimate(
            flops=12 * X * Y * C * (X * T + Z), bytes_accessed=4 * (cells + C * Z), transcendentals=0
        ),
    )(wx, thermal, 16.0 * ky.T, r3)
    return density, thermal_out, fine.reshape(X, Y, Z)


def solution(mesh):
    cells = P("slab", "gy", None)
    in_specs = (cells,) * 5 + (P(), P(), P("gy", None), P(), cells, cells)
    return jax.shard_map(per_device, mesh=mesh, in_specs=in_specs, out_specs=(cells,) * 3, check_vma=False)
```

profile of v0, /device:TPU:0, one launch (start us, length us, event | category | flops | bytes accessed | tf_op | source)
XLA Modules:
  0.0 90.1 jit_solution(12739049548429499690)
XLA Ops:
  0.6 0.9 %add_divide_fusion = f32[8,32,128]{2,1,0:T(8,128)S(1)} fusion(f32[8,32,128]{2,1,0:T(8,128)} %param.20), kind=kLoop, calls=%fused_computation.7 | loop fusion | flops 65536 | bytes 262144 | tf_op jit(solution)/shard_map/div | solution.py:374
  1.6 0.1 copy.45
  1.7 1.0 %copy.44 = f32[1,256,128]{1,0,2:T(1,128)S(1)} copy(f32[1,256,128]{2,1,0:T(8,128)} %bitcast.37) | data formatting | bytes 262144 | tf_op jit(solution)/shard_map/stack | solution.py:374
  2.7 0.2 maximum_bitcast_fusion.1
  2.9 0.1 pad.9
  3.1 0.2 fusion.2
  3.3 0.3 maximum_bitcast_fusion
  3.6 0.0 copy-start.6
  3.7 0.3 copy.46
  3.9 1.3 %copy.47 = f32[32,24,256]{2,1,0:T(8,128)} copy(f32[32,24,256]{2,0,1:T(8,128)S(1)} %bitcast.33) | data formatting | bytes 1572864 | tf_op jit(solution)/shard_map/reshape | solution.py:377
  5.3 7.3 %all-to-all-start = ((f32[32,24,256]{2,1,0:T(8,128)}), f32[32,24,256]{2,1,0:T(8,128)S(1)}, u32[]{:S(2)}, u32[]{:S(2)}) async-start(f32[32,24,256]{2,1,0:T(8,128)} %copy.47), calls=%async_computation | async-start | bytes 1572864 | tf_op jit(solution)/shard_map/all_to_all | solution.py:378
  12.6 0.0 copy-done.6
  12.6 0.0 copy-start
  12.6 0.1 multiply_bitcast_fusion
  12.7 0.3 reshape.43
  13.0 0.0 copy-start.5
  13.0 0.7 slice.30.ky_ref
  13.8 1.0 %copy.55 = f32[256,512]{0,1:T(8,128)} copy(f32[256,512]{1,0:T(8,128)S(1)} %reshape.43) | data formatting | bytes 1048576 | tf_op jit(solution)/shard_map/reshape | solution.py:372
  14.8 0.0 copy-done
  14.8 1.3 %copy.43 = f32[256,1024]{0,1:T(8,128)} copy(f32[256,1024]{1,0:T(8,128)S(1)} %copy-done) | data formatting | bytes 2097152 | tf_op args[8]
  16.1 0.0 copy-done.5
  16.1 0.7 pad_dynamic-slice_fusion.wx_ref
  16.8 40.2 %shard_map.130 = (f32[8,64,1024]{2,1,0:T(8,128)}, f32[10,32,256]{2,1,0:T(8,128)}) custom-call(f32[4]{0:T(128)} %shift_ref.1, f32[6,8]{1,0:T(8,128)} %pad_dynamic-slice_fusion.wx_ref, f32[8,64,1024]{2,1,0:T(8,128)} %volt_hbm.1, f32[8,64,1024]{2,1,0:T(8,128)} %start_hbm.1, f32[8,64,1024]{2,1,0:T(8,128)} %gen_hbm.1, f32[8,64,1024]{2,1,0:T(8,128)} %ann_hbm.1, ...), custom_call_target="tpu_custom_call" | custom-call | flops 104857600 | bytes 12582912 | tf_op jit(solution)/shard_map/pallas_call | solution.py:390
  57.0 0.0 all-to-all-done
  57.0 2.3 %reshape.46 = f32[32,24,8,32]{3,2,1,0:T(8,128)} reshape(f32[32,24,256]{2,1,0:T(8,128)S(1)} %all-to-all-done) | data formatting | bytes 1572864 | tf_op jit(solution)/shard_map/reshape | solution.py:379
  59.4 2.1 %fusion.1 = (f32[12,32,32,8]{1,3,0,2:T(8,128)S(1)}, f32[12,32,32,8]{1,3,0,2:T(8,128)S(1)}) fusion(f32[24,32,32,8]{1,3,0,2:T(8,128)} %bitcast.30), kind=kLoop, calls=%fused_computation.10 | loop fusion | bytes 1572864 | tf_op jit(solution)/shard_map/slice | solution.py:419
  61.5 1.5 %copy_bitcast_fusion = (f32[12,32,256]{1,2,0:T(8,128)}, f32[12,32,256]{1,2,0:T(8,128)S(1)}) fusion(f32[12,32,32,8]{1,3,0,2:T(8,128)S(1)} %get-tuple-element.10, f32[12,32,32,8]{1,3,0,2:T(8,128)S(1)} %get-tuple-element.11), kind=kLoop, calls=%fused_computation | loop fusion | bytes 1572864 | tf_op jit(solution)/shard_map/squeeze | solution.py:419
  63.0 2.6 %copy.51.rc_ref = f32[12,32,256]{2,1,0:T(8,128)} copy(f32[12,32,256]{1,2,0:T(8,128)} %get-tuple-element.15) | data formatting | bytes 786432 | tf_op jit(solution)/shard_map/squeeze | solution.py:419
  65.6 1.2 %copy.50.start_ref = f32[12,32,256]{2,1,0:T(8,128)} copy(f32[12,32,256]{1,2,0:T(8,128)S(1)} %get-tuple-element.16) | data formatting | bytes 786432 | tf_op jit(solution)/shard_map/squeeze | solution.py:419
  66.8 0.0 copy-start.4
  66.8 0.0 copy-start.2
  66.8 2.5 %shard_map.131.t_ref = f32[6,32,256]{2,1,0:T(8,128)} custom-call(f32[10,32,256]{2,1,0:T(8,128)} %get-tuple-element.6.src_ref, f32[12,32,256]{2,1,0:T(8,128)} %copy.50.start_ref, f32[12,32,256]{2,1,0:T(8,128)} %copy.51.rc_ref), custom_call_target="tpu_custom_call" | custom-call | tf_op jit(solution)/shard_map/pallas_call | solution.py:413
  69.2 0.0 copy-start.1
  69.2 1.0 %slice.36 = f32[4,32,256]{2,1,0:T(8,128)S(1)} slice(f32[6,32,256]{2,1,0:T(8,128)} %shard_map.131.t_ref), slice={[1:5], [0:32], [0:256]} | slice | bytes 262144 | tf_op jit(solution)/shard_map/slice | solution.py:433
  70.2 0.2 copy.52
  70.4 0.2 reshape.48
  70.6 0.7 copy.53
  71.4 8.4 %all-to-all-start.1 = ((f32[32,4,256]{2,1,0:T(4,128)}), f32[32,4,256]{2,1,0:T(4,128)S(1)}, u32[]{:S(2)}, u32[]{:S(2)}) async-start(f32[32,4,256]{2,1,0:T(4,128)} %copy.53), calls=%async_computation.1 | async-start | bytes 262144 | tf_op jit(solution)/shard_map/all_to_all | solution.py:434
  79.8 0.0 copy-done.4
  79.8 0.0 copy-done.2
  79.8 0.0 copy-done.1
  79.8 0.0 copy-start.3
  79.9 4.9 %shard_map.132 = f32[512,1024]{1,0:T(8,128)} custom-call(f32[6,8]{1,0:T(8,128)S(1)} %copy-done.2, f32[6,32,256]{2,1,0:T(8,128)S(1)} %copy-done.1, f32[512,256]{1,0:T(8,128)S(1)} %multiply_bitcast_fusion.1.ky_ref, f32[256,1024]{1,0:T(8,128)S(1)} %copy-done), custom_call_target="tpu_custom_call" | custom-call | flops 2013265920 | bytes 3145728 | tf_op jit(solution)/shard_map/pallas_call | solution.py:438
  84.8 3.2 %all-to-all-done.1 = f32[32,4,256]{2,1,0:T(4,128)S(1)} async-done(((f32[32,4,256]{2,1,0:T(4,128)}), f32[32,4,256]{2,1,0:T(4,128)S(1)}, u32[]{:S(2)}, u32[]{:S(2)}) %all-to-all-start.1) | async-done | bytes 131104 | tf_op jit(solution)/shard_map/all_to_all | solution.py:434
  88.0 0.8 copy.54
  88.8 0.0 copy-done.3
  88.8 1.3 %copy.59 = f32[8,64,1024]{2,1,0:T(8,128)} copy(f32[8,64,1024]{2,1,0:T(8,128)S(1)} %copy-done.3) | data formatting | bytes 4194304
  (3 shorter events, 0.1 us)
Async XLA Ops:
  3.6 8.9 %copy-start.6 = (f32[32,64]{1,0:T(8,128)S(1)}, f32[32,64]{1,0:T(8,128)}, u32[]{:S(2)}) copy-start(f32[32,64]{1,0:T(8,128)} %param.18) | copy-start | bytes 24580
  5.3 51.7 %all-to-all-start = ((f32[32,24,256]{2,1,0:T(8,128)}), f32[32,24,256]{2,1,0:T(8,128)S(1)}, u32[]{:S(2)}, u32[]{:S(2)}) async-start(f32[32,24,256]{2,1,0:T(8,128)} %copy.47), calls=%async_computation | async-start | bytes 1572864 | tf_op jit(solution)/shard_map/all_to_all | solution.py:378
  12.6 2.2 %copy-start = (f32[256,1024]{1,0:T(8,128)S(1)}, f32[256,1024]{1,0:T(8,128)}, u32[]{:S(2)}) copy-start(f32[256,1024]{1,0:T(8,128)} %r3_ref.1) | copy-start | bytes 3145732
  13.0 3.1 %copy-start.5 = (f32[128,256]{1,0:T(8,128)S(1)}, f32[128,256]{1,0:T(8,128)}, u32[]{:S(2)}) copy-start(f32[128,256]{1,0:T(8,128)} %param.17) | copy-start | bytes 393220
  66.8 13.0 %copy-start.4 = (f32[256,512]{0,1:T(8,128)S(1)}, f32[256,512]{0,1:T(8,128)}, u32[]{:S(2)}) copy-start(f32[256,512]{0,1:T(8,128)} %copy.55) | copy-start | bytes 1572868
  66.8 13.1 %copy-start.2 = (f32[6,8]{1,0:T(8,128)S(1)}, f32[6,8]{1,0:T(8,128)}, u32[]{:S(2)}) copy-start(f32[6,8]{1,0:T(8,128)} %pad_dynamic-slice_fusion.wx_ref) | copy-start | bytes 580
  69.2 10.6 %copy-start.1 = (f32[6,32,256]{2,1,0:T(8,128)S(1)}, f32[6,32,256]{2,1,0:T(8,128)}, u32[]{:S(2)}) copy-start(f32[6,32,256]{2,1,0:T(8,128)} %shard_map.131.t_ref) | copy-start | bytes 589828
  71.4 16.6 %all-to-all-start.1 = ((f32[32,4,256]{2,1,0:T(4,128)}), f32[32,4,256]{2,1,0:T(4,128)S(1)}, u32[]{:S(2)}, u32[]{:S(2)}) async-start(f32[32,4,256]{2,1,0:T(4,128)} %copy.53), calls=%async_computation.1 | async-start | bytes 262144 | tf_op jit(solution)/shard_map/all_to_all | solution.py:434
  79.8 9.0 %copy-start.3 = (f32[8,64,1024]{2,1,0:T(8,128)S(1)}, f32[8,64,1024]{2,1,0:T(8,128)}, u32[]{:S(2)}) copy-start(f32[8,64,1024]{2,1,0:T(8,128)} %get-tuple-element.20) | copy-start | bytes 6291460
where the time goes:
time: 90.5 us; the launch traced here: 90.1 us
  Pallas kernels  47.6 us (53%)
  local copies, waits for them, and re-layouts  21.1 us (23%)
  starting transfers between devices  15.7 us (17%)
  waiting for transfers between devices  3.25 us (4%)
  other arithmetic  1.69 us (2%)
    pallas_call x1, Pallas kernels, per_device(): pl.pallas_call(functools.partial(device_kernel, slabs, yblocks), out_shap...  40.2 us
    all_to_all x1, starting transfers between devices, per_device(): mine = lax.all_to_all(mine, 'slab', 0, 0, tiled=True).reshape(AT, CL * T)  8.4 us
    all_to_all x1, starting transfers between devices, per_device(): both = lax.all_to_all(both, 'slab', 0, 0, tiled=True)  7.3 us
    pallas_call x1, Pallas kernels, per_device(): pl.pallas_call(prolong_kernel, grid=(steps,), out_shape=jax.ShapeDtypeStr...  4.9 us
    squeeze x2, local copies, waits for them, and re-layouts, per_device(): both[1]  4.1 us
    all_to_all x1, waiting for transfers between devices, per_device(): mine = lax.all_to_all(mine, 'slab', 0, 0, tiled=True).reshape(AT, CL * T)  3.24 us
    unnamed x16, local copies, waits for them, and re-layouts  2.66 us
    pallas_call x1, Pallas kernels, per_device(): pl.pallas_call(thermal_kernel, out_shape=jax.ShapeDtypeStruct((A + 2, T,...  2.48 us
  transfers between devices with their start and end apart: 2, of which 1 were waited for; matrix products, arithmetic and copies ran while one was open for 5% of the time, Pallas kernels for 50%

commit v1 on v0

--- a/solution.py
+++ b/solution.py
@@ -15,25 +15,36 @@
 MIB = 1024 * 1024
 
 
+def inverse(v):
+    r = pl.reciprocal(v, approx=True)
+    return r * (2.0 - v * r)
+
+
 def bernoulli(u):
     small = jnp.abs(u) < 0.03125
     series = 1.0 + u * (u * (1.0 / 12.0) - 0.5)
-    return jnp.where(small, series, u / (jnp.exp(u) - 1.0))
+    return jnp.where(small, series, u * inverse(jnp.exp(u) - 1.0))
+
+
+def product(a, b, dims=((1,), (0,))):
+    return lax.dot_general(a, b, (dims, ((), ())), precision=HIGHEST, preferred_element_type=jnp.float32)
 
 
 def device_kernel(
     slabs, yblocks,
-    shift_ref, wx_ref, volt_hbm, start_hbm, gen_hbm, ann_hbm, grain_hbm, r3t_hbm, ky_ref,
-    dens_hbm, src_ref,
-    E, N0, N1, N2, GEN, ANN, GR, RD, BX, MX, BY, MY, BZ, MZ, B0, U0, HEAT, R3T, HZ, SEND, GOTL, GOTR,
-    in_sem, out_sem, send_sem, recv_sem,
+    shift_ref, volt_hbm, start_hbm, gen_hbm, ann_hbm, grain_hbm, r3_hbm, *rest
 ):
+    count = 4 if yblocks == 1 else 2
+    extra_in, rest = rest[:count], rest[count:]
+    count = 3 if yblocks == 1 else 2
+    (dens_hbm, *extra_out), rest = rest[:count], rest[count:]
+    (E, N0, N1, N2, GEN, ANN, GR, RD, BX, MX, BY, MY, BZ, MZ, B0, U0, HEAT, R3,
+     in_sem, out_sem, send_sem, recv_sem, *extra) = rest
     X, Y, Z = GEN.shape
     me = lax.axis_index("slab")
     gy = lax.axis_index("gy")
     rows = slice(PAD, PAD + Y)
     chunks = range(0, Y, 8)
-    t_rows = src_ref.shape[1]
 
     loads = {}
 
@@ -52,7 +63,7 @@
     load("a", ann_hbm, ANN)
     load("n", start_hbm.at[inner], N0.at[pl.ds(2, X - 2), pl.ds(PAD, Y)])
     load("gen", gen_hbm, GEN)
-    load("r3t", r3t_hbm, R3T)
+    load("r3", r3_hbm, R3)
 
     zero_rows = jnp.zeros((X + 2, PAD, Z), jnp.float32)
     zero_layer = jnp.zeros((Y, Z), jnp.float32)
@@ -68,24 +79,72 @@
         def _():
             buf[X + 1, rows, :] = zero_layer
 
-    @pl.when(me == 0)
-    def _():
-        GOTL[...] = jnp.zeros_like(GOTL)
-
-    @pl.when(me == slabs - 1)
-    def _():
-        GOTR[...] = jnp.zeros_like(GOTR)
+    def others(body):
+        def step(i, carry):
+            body(lax.rem(me + i, slabs))
+            return carry
+        lax.fori_loop(1, slabs, step, 0)
+
+    if yblocks == 1:
+        warm_ref, cool_ref, r2_tile, wx_rows = extra_in
+        fine_hbm, thermal_ref = extra_out
+        P, TRC, TR, SRC, W, SL, SR, GOTL, GOTR, OWN, RCV, all_send, all_recv = extra
+        CL, T, AT = warm_ref.shape
+        A = AT // slabs
+        AW = A * T
+        group = 128 // T
+        low, mid, high = slice(0, AW), slice(AW, 2 * AW), slice(2 * AW, 3 * AW)
+
+        for k in range(2):
+            for c0 in range(0, CL, group):
+                v = (warm_ref if k == 0 else cool_ref)[c0:c0 + group].reshape(group * T, AT)
+                TR[...] = (v if k == 0 else 1.0 / (6.0 + v)).T
+                cols = [TR[pl.ds(j, slabs, stride=A), :] for j in range(A)]
+                for c in range(group):
+                    P[k, pl.ds(c0 + c, slabs, stride=CL), :] = jnp.concatenate(
+                        [v[:, c * T:(c + 1) * T] for v in cols], axis=1
+                    )
+
+        def slab_rows(d):
+            return pl.ds(pl.multiple_of(d * CL, CL), CL)
+
+        TRC[:, slab_rows(me), mid] = P[:, slab_rows(me), :]
+
+        @pl.when(me == 0)
+        def _():
+            GOTL[...] = jnp.zeros_like(GOTL)
+            TRC[:, :, low] = jnp.zeros((2, CL * slabs, AW), jnp.float32)
+
+        @pl.when(me == slabs - 1)
+        def _():
+            GOTR[...] = jnp.zeros_like(GOTR)
+            TRC[:, :, high] = jnp.zeros((2, CL * slabs, AW), jnp.float32)
+    else:
+        SEND, HZ, GOTL, GOTR = extra
+        wx_ref, ky_ref = extra_in
+
+        @pl.when(me == 0)
+        def _():
+            GOTL[...] = jnp.zeros_like(GOTL)
+
+        @pl.when(me == slabs - 1)
+        def _():
+            GOTR[...] = jnp.zeros_like(GOTR)
 
     x_sides = [(me > 0, (me - 1, gy)), (me < slabs - 1, (me + 1, gy))]
     y_sides = [] if yblocks == 1 else [(gy > 0, (me, gy - 1)), (gy < yblocks - 1, (me, gy + 1))]
 
     barrier = pltpu.get_barrier_semaphore()
-    for has, device in x_sides + y_sides:
-        @pl.when(has)
-        def _():
-            pl.semaphore_signal(barrier, inc=1, device_id=device, device_id_type=MESH)
-    peers = sum(has.astype(jnp.int32) for has, _ in x_sides + y_sides)
-    pl.semaphore_wait(barrier, peers)
+    if yblocks == 1:
+        others(lambda d: pl.semaphore_signal(barrier, inc=1, device_id=(d, gy), device_id_type=MESH))
+        pl.semaphore_wait(barrier, slabs - 1)
+    else:
+        for has, device in x_sides + y_sides:
+            @pl.when(has)
+            def _():
+                pl.semaphore_signal(barrier, inc=1, device_id=device, device_id_type=MESH)
+        peers = sum(has.astype(jnp.int32) for has, _ in x_sides + y_sides)
+        pl.semaphore_wait(barrier, peers)
 
     def side_copy(slot, d, device, src, dst):
         return pltpu.make_async_remote_copy(
@@ -155,6 +214,18 @@
         loads[("n", layer)].wait()
     n_copies = x_copies(1, N0)
     start(n_copies)
+
+    def all_copy(k, src, dst, d, s):
+        return pltpu.make_async_remote_copy(
+            src_ref=src, dst_ref=dst, send_sem=all_send.at[k, d], recv_sem=all_recv.at[k, s],
+            device_id=(d, gy), device_id_type=MESH,
+        )
+
+    if yblocks == 1:
+        def spread_copy(d, s):
+            return all_copy(0, P.at[:, slab_rows(d)], TRC.at[:, slab_rows(s), pl.ds(AW, AW)], d, s)
+
+        others(lambda d: spread_copy(d, me).start())
     loads["v"].wait()
     loads["g"].wait()
     over_layers(1, X - 1, effective)
@@ -165,15 +236,16 @@
     loads["a"].wait()
 
     lane = lax.broadcasted_iota(jnp.int32, (8, Z), 1)
-    first_lane = lane == 0
     last_lane = lane == Z - 1
-    lane0 = lax.broadcasted_iota(jnp.int32, (8, 128), 1) == 0
+    edge = lax.broadcasted_iota(jnp.int32, (8, 128), 1)
+    lane0, lane1 = edge == 0, edge == 127
+    head, tail = slice(0, 128), slice(Z - 128, Z)
 
     def up_z(v):
-        return jnp.where(last_lane, 0.0, pltpu.roll(v, Z - 1, 1))
+        return pltpu.roll(v, Z - 1, 1)
 
     def down_z(v):
-        return jnp.where(first_lane, 0.0, pltpu.roll(v, 1, 1))
+        return pltpu.roll(v, 1, 1)
 
     def yz_faces(x):
         u = E[x + 1, PAD:PAD + 8, :] - E[x + 1, PAD - 1:PAD + 7, :]
@@ -190,15 +262,17 @@
             MY[x, r:r + 8, :] = my
             uz = up_z(e) - e
             bz = bernoulli(uz)
-            mz = bz + uz
+            mz = jnp.where(last_lane, 0.0, bz + uz)
+            bz = jnp.where(last_lane, 0.0, bz)
             BZ[x, y:y + 8, :] = bz
             MZ[x, y:y + 8, :] = mz
-            e0 = e[:, 0:128]
+            e0 = jnp.where(lane0, e[:, head], e[:, tail])
             b0 = bernoulli(e0)
-            B0[x, y:y + 8, :] = jnp.where(lane0, b0, 0.0)
-            U0[x, y:y + 8, :] = jnp.where(lane0, 0.5 * e0 * b0, 0.0)
-            RD[x, y:y + 8, :] = ANN[x, y:y + 8, :] + my + mz + down_z(bz) + BY[x, r - 1:r + 7, :]
-            RD[x, y:y + 8, 0:128] = RD[x, y:y + 8, 0:128] + B0[x, y:y + 8, :]
+            U0[x, y:y + 8, :] = 0.5 * e0 * b0
+            total = ANN[x, y:y + 8, :] + my + mz + down_z(bz) + BY[x, r - 1:r + 7, :]
+            RD[x, y:y + 8, :] = total
+            RD[x, y:y + 8, head] = total[:, head] + jnp.where(lane0, b0, 0.0)
+            RD[x, y:y + 8, tail] = total[:, tail] + jnp.where(lane1, b0, 0.0)
 
     over_layers(0, X, yz_faces)
 
@@ -216,6 +290,12 @@
     x_face(X)
     loads["gen"].wait()
     finish(n_copies)
+    if yblocks == 1:
+        others(lambda s: spread_copy(s, s).wait_recv())
+        block_copies = [
+            (has, side_copy(5, d, device, TRC.at[:, :, pl.ds(AW, AW)], TRC.at[:, :, pl.ds(2 * AW if d == 0 else 0, AW)]))
+            for d, (has, device) in enumerate(x_sides)
+        ]
 
     def sweep(src, dst, first):
         def layer(x):
@@ -228,7 +308,7 @@
                 total = total + MY[x, r - 1:r + 7, :] * src[x + 1, r - 1:r + 7, :]
                 total = total + BZ[x, c, :] * up_z(n) + down_z(MZ[x, c, :] * n)
                 if first:
-                    rd = 1.0 / (RD[x, c, :] + MX[x + 1, c, :] + BX[x, c, :])
+                    rd = inverse(RD[x, c, :] + MX[x + 1, c, :] + BX[x, c, :])
                     RD[x, c, :] = rd
                 else:
                     rd = RD[x, c, :]
@@ -240,6 +320,8 @@
     over_layers(X - 1, X, first)
     one_copies = x_copies(2, N1)
     start(one_copies)
+    if yblocks == 1:
+        start(block_copies)
     over_layers(1, X - 1, first)
     if y_sides:
         exchange_y(2, N1)
@@ -255,6 +337,66 @@
     if y_sides:
         exchange_y(3, N2)
 
+    def solve_and_prolong():
+        for x in range(X):
+            W[x * Y:(x + 1) * Y, :] = r2_tile[...] * wx_rows[x:x + 1, :]
+        along_z = product(R3[...], HEAT[...].reshape(X * Y, Z), ((1,), (1,)))
+        SL[...] = product(along_z, W[:, AW - T:2 * AW - T])
+        SR[...] = product(along_z, W[:, AW + T:2 * AW + T])
+        copies = [
+            (has, side_copy(4, d, device, SL if d == 0 else SR, GOTR if d == 0 else GOTL))
+            for d, (has, device) in enumerate(x_sides)
+        ]
+        start(copies)
+
+        def zeros(columns):
+            return jnp.zeros((CL * slabs, columns * T), jnp.float32)
+
+        SRC[...] = jnp.concatenate([zeros(A - 1), SL[...], zeros(A + 1)], axis=1)
+        SRC[:, 2 * AW - T:2 * AW + T] = SRC[:, 2 * AW - T:2 * AW + T] + SR[:, AW - 2 * T:]
+        finish(copies)
+        SRC[...] = (
+            SRC[...] + jnp.concatenate([zeros(1), GOTL[...], zeros(2 * A - 1)], axis=1)
+            + jnp.concatenate([zeros(2 * A - 1), GOTR[...], zeros(1)], axis=1)
+        )
+        C = CL * slabs
+        row = lax.broadcasted_iota(jnp.int32, (C, 3 * AW), 0)
+        cell = lax.rem(lax.broadcasted_iota(jnp.int32, (C, 3 * AW), 1), T)
+        for _ in range(HEAT_SWEEPS):
+            v = TRC[0]
+            total = SRC[...] + pltpu.roll(v, T, 1) + pltpu.roll(v, 3 * AW - T, 1)
+            total = total + jnp.where(row == 0, 0.0, pltpu.roll(v, 1, 0))
+            total = total + jnp.where(row == C - 1, 0.0, pltpu.roll(v, C - 1, 0))
+            total = total + jnp.where(cell == 0, 0.0, pltpu.roll(v, 1, 1))
+            total = total + jnp.where(cell == T - 1, 0.0, pltpu.roll(v, 3 * AW - 1, 1))
+            TRC[0] = total * TRC[1]
+        OWN[...] = TRC[0, :, mid]
+
+        def back_copy(d, s):
+            return all_copy(1, OWN.at[slab_rows(d)], RCV.at[slab_rows(s)], d, s)
+
+        others(lambda d: back_copy(d, me).start())
+        RCV[slab_rows(me), :] = OWN[slab_rows(me), :]
+        spread = 16.0 * product(W[:, AW - T:2 * AW + T], TRC[0, :, AW - T:2 * AW + T], ((1,), (1,)))
+        writes = []
+        for x in range(0, X, 2):
+            HEAT[x:x + 2] = product(spread[x * Y:(x + 2) * Y], R3[...]).reshape(2, Y, Z)
+            writes.append(pltpu.make_async_copy(
+                HEAT.at[pl.ds(x, 2)], fine_hbm.at[pl.ds(x, 2)], in_sem.at[len(loads) + len(writes)]
+            ))
+            writes[-1].start()
+        others(lambda s: back_copy(s, s).wait_recv())
+        for c0 in range(0, CL, group):
+            cols = [RCV[pl.ds(c0 + c, slabs, stride=CL), :] for c in range(group)]
+            for j in range(A):
+                TR[pl.ds(j, slabs, stride=A), :] = jnp.concatenate(
+                    [v[:, j * T:(j + 1) * T] for v in cols], axis=1
+                )
+            thermal_ref[c0:c0 + group] = TR[...].T.reshape(group, T, AT)
+        others(lambda d: back_copy(d, me).wait_send())
+        for write in writes:
+            write.wait()
+
     def heat(x):
         for y in chunks:
             r = PAD + y
@@ -272,18 +414,25 @@
             )
             fz = term(BZ[x, c, :], MZ[x, c, :], n, up_z(n))
             total = total + fz + down_z(fz)
-            HEAT[x, c, :] = 0.5 * total
-            HEAT[x, c, 0:128] = HEAT[x, c, 0:128] + U0[x, c, :] * n[:, 0:128]
+            total = 0.5 * total
+            HEAT[x, c, :] = total
+            u0 = U0[x, c, :]
+            HEAT[x, c, head] = total[:, head] + jnp.where(lane0, u0 * n[:, head], 0.0)
+            HEAT[x, c, tail] = total[:, tail] + jnp.where(lane1, u0 * n[:, tail], 0.0)
 
     over_layers(1, X - 1, heat)
     finish(two_copies)
     over_layers(0, 1, heat)
     over_layers(X - 1, X, heat)
 
-    loads["r3t"].wait()
-    HZ[...] = jnp.dot(
-        HEAT[...].reshape(X * Y, Z), R3T[...], precision=HIGHEST, preferred_element_type=jnp.float32
-    ).reshape(HZ.shape)
+    loads["r3"].wait()
+    if yblocks == 1:
+        finish(block_copies)
+        others(lambda d: spread_copy(d, me).wait_send())
+        solve_and_prolong()
+        out.wait()
+        return
+    HZ[...] = product(HEAT[...].reshape(X * Y, Z), R3[...], ((1,), (1,))).reshape(HZ.shape)
     A = X // 2
     parts = []
     for a in range(A + 2):
@@ -298,6 +447,7 @@
     SEND[...] = share.reshape(SEND.shape)
     has_l, left = x_sides[0]
     has_r, right = x_sides[1]
+    src_ref, = extra_out
     copies = [
         (has_l, side_copy(4, 0, left, SEND.at[pl.ds(0, A)], GOTR)),
         (has_r, side_copy(4, 1, right, SEND.at[pl.ds(2, A)], GOTL)),
@@ -314,29 +464,6 @@
     out.wait()
 
 
-def thermal_kernel(src_ref, start_ref, rc_ref, out_ref, ta, tb):
-    A = out_ref.shape[0] - 2
-    T, C = out_ref.shape[1:]
-    row = lax.broadcasted_iota(jnp.int32, (T, C), 0)
-    col = lax.broadcasted_iota(jnp.int32, (T, C), 1)
-    bufs = [start_ref, ta, tb, None]
-    width = start_ref.shape[0]
-    for sweep in range(HEAT_SWEEPS):
-        old = bufs[sweep]
-        for a in range(sweep + 1, width - 1 - sweep):
-            v = old[a]
-            total = src_ref[a - 1] + old[a - 1] + old[a + 1]
-            total = total + jnp.where(row == T - 1, 0.0, pltpu.roll(v, T - 1, 0))
-            total = total + jnp.where(row == 0, 0.0, pltpu.roll(v, 1, 0))
-            total = total + jnp.where(col == C - 1, 0.0, pltpu.roll(v, C - 1, 1))
-            total = total + jnp.where(col == 0, 0.0, pltpu.roll(v, 1, 1))
-            new = total * rc_ref[a]
-            if sweep == HEAT_SWEEPS - 1:
-                out_ref[a - HEAT_SWEEPS] = new
-            else:
-                bufs[sweep + 1][a] = new
-
-
 def prolong_kernel(wx_ref, t_ref, ky_ref, r3_ref, out_ref, spread):
     X = wx_ref.shape[1]
     A = X // 2
@@ -368,16 +495,6 @@
     f32 = jnp.float32
 
     wx = lax.dynamic_slice(jnp.pad(r1, ((1, 1), (0, 0))), (me * A, me * X), (A + 2, X))
-    eye = jnp.eye(X, dtype=f32)
-    ky = jnp.einsum("ij,tc->itjc", eye, r2, precision=HIGHEST).reshape(X * T, X * Y)
-
-    both = jnp.stack([warming, 1.0 / (6.0 + cooling)]).reshape(2, CL * T, AT)
-    both = jnp.pad(both.transpose(0, 2, 1), ((0, 0), (A, A), (0, 0))).reshape(2, slabs + 2, A, CL * T)
-    both = jnp.concatenate([both[:, i:i + slabs] for i in range(3)], axis=2)
-    both = both.transpose(1, 0, 2, 3).reshape(slabs, 6 * A, CL * T)
-    both = lax.all_to_all(both, "slab", 0, 0, tiled=True)
-    both = both.reshape(slabs, 6 * A, CL, T).transpose(1, 3, 0, 2).reshape(2, 3 * A, T, C)
-
     smem = pl.BlockSpec(memory_space=pltpu.SMEM)
     vmem = pl.BlockSpec(memory_space=pltpu.VMEM)
     anyspace = pl.BlockSpec(memory_space=pl.ANY)
@@ -387,48 +504,68 @@
     yface = pltpu.VMEM((X, Y + PAD, Z), f32)
     edge = pltpu.VMEM((X, Y, 128), f32)
     cells = X * Y * Z
-    density, source = pl.pallas_call(
+    scratch = [
+        padded, padded, padded, padded, block, block, pltpu.VMEM((X, Y, Z), jnp.int32), block,
+        xface, xface, yface, yface, block, block, edge, edge, block, pltpu.VMEM((C, Z), f32),
+        pltpu.SemaphoreType.DMA((20,)), pltpu.SemaphoreType.DMA,
+        pltpu.SemaphoreType.DMA((6, 4)), pltpu.SemaphoreType.DMA((6, 4)),
+    ]
+    full = jax.ShapeDtypeStruct((X, Y, Z), f32)
+    call = functools.partial(
+        pl.pallas_call,
         functools.partial(device_kernel, slabs, yblocks),
-        out_shape=(
-            jax.ShapeDtypeStruct((X, Y, Z), f32),
-            jax.ShapeDtypeStruct((3 * A - 2, T, C), f32),
-        ),
-        in_specs=[smem, smem] + [anyspace] * 6 + [vmem],
-        out_specs=(anyspace, vmem),
-        scratch_shapes=[
-            padded, padded, padded, padded, block, block, pltpu.VMEM((X, Y, Z), jnp.int32), block,
-            xface, xface, yface, yface, block, block, edge, edge, block,
-            pltpu.VMEM((Z, C), f32), pltpu.VMEM((X, Y, C), f32), pltpu.VMEM((A + 2, T, C), f32),
-            pltpu.VMEM((A, T, C), f32), pltpu.VMEM((A, T, C), f32),
-            pltpu.SemaphoreType.DMA((16,)), pltpu.SemaphoreType.DMA,
-            pltpu.SemaphoreType.DMA((5, 4)), pltpu.SemaphoreType.DMA((5, 4)),
-        ],
         compiler_params=pltpu.CompilerParams(
             collective_id=0, has_side_effects=True, vmem_limit_bytes=58 * MIB
         ),
-        cost_estimate=pl.CostEstimate(flops=200 * cells, bytes_accessed=24 * cells, transcendentals=3 * cells),
-    )(barrier_shift, wx, volt, start, gen, ann, grain, r3.T, ky[:(A + 2) * T, :(A + 2) * Y])
-
-    if yblocks == 1:
-        thermal = pl.pallas_call(
-            thermal_kernel,
-            out_shape=jax.ShapeDtypeStruct((A + 2, T, C), f32),
-            in_specs=[vmem] * 3,
-            out_specs=vmem,
-            scratch_shapes=[pltpu.VMEM((3 * A, T, C), f32)] * 2,
-        )(source, both[0], both[1])
-    else:
-        thermal = both[0]
-        up = [(i, i + 1) for i in range(yblocks - 1)]
-        down = [(i + 1, i) for i in range(yblocks - 1)]
-        for sweep in range(HEAT_SWEEPS):
-            low = lax.ppermute(thermal[:, -1:], "gy", up)
-            high = lax.ppermute(thermal[:, :1], "gy", down)
-            tall = jnp.concatenate([low, thermal, high], axis=1)
-            wide = jnp.pad(thermal, ((0, 0), (0, 0), (1, 1)))
-            total = source[sweep:3 * A - 2 - sweep] + thermal[2:] + thermal[:-2]
-            total = total + (tall[:, 2:] + tall[:, :-2] + wide[:, :, 2:] + wide[:, :, :-2])[1:-1]
-            thermal = total * both[1][sweep + 1:3 * A - 1 - sweep]
+        cost_estimate=pl.CostEstimate(flops=200 * cells, bytes_accessed=28 * cells, transcendentals=3 * cells),
+    )
+    operands = (barrier_shift, volt, start, gen, ann, grain, r3)
+
+    if yblocks == 1:
+        AW = A * T
+        wx_rows = jnp.pad(wx.T, ((0, 0), (A - 1, A - 1)))
+        wx_rows = jnp.repeat(wx_rows, T, axis=1)
+        density, fine, thermal_out = call(
+            out_shape=(full, full, jax.ShapeDtypeStruct((CL, T, AT), f32)),
+            in_specs=[smem] + [anyspace] * 6 + [vmem] * 4,
+            out_specs=(anyspace, anyspace, vmem),
+            scratch_shapes=scratch + [
+                pltpu.VMEM((2, C, AW), f32), pltpu.VMEM((2, C, 3 * AW), f32), pltpu.VMEM((AT, 128), f32),
+                pltpu.VMEM((C, 3 * AW), f32), pltpu.VMEM((X * Y, 3 * AW), f32),
+            ] + [pltpu.VMEM((C, AW), f32)] * 6 + [pltpu.SemaphoreType.DMA((2, slabs))] * 2,
+        )(*operands, warming, cooling, jnp.tile(r2.T, (1, 3 * A)), wx_rows)
+        return density, thermal_out, fine
+
+    eye = jnp.eye(X, dtype=f32)
+    ky = jnp.einsum("ij,tc->itjc", eye, r2, precision=HIGHEST).reshape(X * T, X * Y)
+    both = jnp.stack([warming, 1.0 / (6.0 + cooling)]).reshape(2, CL * T, AT)
+    both = jnp.pad(both.transpose(0, 2, 1), ((0, 0), (A, A), (0, 0))).reshape(2, slabs + 2, A, CL * T)
+    both = jnp.concatenate([both[:, i:i + slabs] for i in range(3)], axis=2)
+    both = both.transpose(1, 0, 2, 3).reshape(slabs, 6 * A, CL * T)
+    both = lax.all_to_all(both, "slab", 0, 0, tiled=True)
+    both = both.reshape(slabs, 6 * A, CL, T).transpose(1, 3, 0, 2).reshape(2, 3 * A, T, C)
+
+    density, source = call(
+        out_shape=(full, jax.ShapeDtypeStruct((3 * A - 2, T, C), f32)),
+        in_specs=[smem] + [anyspace] * 6 + [smem, vmem],
+        out_specs=(anyspace, vmem),
+        scratch_shapes=scratch + [
+            pltpu.VMEM((A + 2, T, C), f32), pltpu.VMEM((X, Y, C), f32),
+            pltpu.VMEM((A, T, C), f32), pltpu.VMEM((A, T, C), f32),
+        ],
+    )(*operands, wx, ky[:(A + 2) * T, :(A + 2) * Y])
+
+    thermal = both[0]
+    up = [(i, i + 1) for i in range(yblocks - 1)]
+    down = [(i + 1, i) for i in range(yblocks - 1)]
+    for sweep in range(HEAT_SWEEPS):
+        low = lax.ppermute(thermal[:, -1:], "gy", up)
+        high = lax.ppermute(thermal[:, :1], "gy", down)
+        tall = jnp.concatenate([low, thermal, high], axis=1)
+        wide = jnp.pad(thermal, ((0, 0), (0, 0), (1, 1)))
+        total = source[sweep:3 * A - 2 - sweep] + thermal[2:] + thermal[:-2]
+        total = total + (tall[:, 2:] + tall[:, :-2] + wide[:, :, 2:] + wide[:, :, :-2])[1:-1]
+        thermal = total * both[1][sweep + 1:3 * A - 1 - sweep]
 
     mine = thermal[1:A + 1].reshape(A, T, slabs, CL).transpose(2, 0, 3, 1).reshape(slabs, A, CL * T)
     mine = lax.all_to_all(mine, "slab", 0, 0, tiled=True).reshape(AT, CL * T)

time: 90.5 us -> 71.1 us (0.79)
  starting transfers between devices: 15.7 us -> 0 us
  Pallas kernels: 47.6 us -> 61.6 us
  local copies, waits for them, and re-layouts: 21.1 us -> 8.49 us
  waiting for transfers between devices: 3.25 us -> 0 us
  other arithmetic: 1.69 us -> 0 us
    all_to_all x2 -> x0, starting transfers between devices: 15.7 us -> none  [the longest x1 8.4 us: per_device(): mine = lax.all_to_all(mine, 'slab', 0, 0, tiled=True).reshape(AT, CL * T)]
    pallas_call x3 -> x1, Pallas kernels: 47.6 us -> 61.6 us  [per_device(): call(out_shape=(full, full, jax.ShapeDtypeStruct((CL, T, AT), f32)), in_s...]
    squeeze x3 -> x0, local copies, waits for them, and re-layouts: 5.29 us -> none  [the longest x2 4.1 us: per_device(): both[1]]
    reshape x7 -> x1, local copies, waits for them, and re-layouts: 5.96 us -> 0.69 us  [per_device(): wx_rows = jnp.repeat(wx_rows, T, axis=1)]
    slice x5 -> x0, local copies, waits for them, and re-layouts: 4.24 us -> none  [the longest x1 2.09 us: per_device(): both[1]]
    all_to_all x2 -> x0, waiting for transfers between devices: 3.25 us -> none  [the longest x1 3.24 us: per_device(): mine = lax.all_to_all(mine, 'slab', 0, 0, tiled=True).reshape(AT, CL * T)]
    unnamed x16 -> x8, local copies, waits for them, and re-layouts: 2.66 us -> 5.38 us
    div x1 -> x0, other arithmetic: 0.93 us -> none  [per_device(): both = jnp.stack([warming, 1.0 / (6.0 + cooling)]).reshape(2, CL * T, AT)]
  transfers between devices with their start and end apart: 2 -> 0, of which waited for: 1 -> 0; matrix products, arithmetic and copies ran while one was open for 5% -> 0% of each run, Pallas kernels for 50% -> 0%
where the time goes in v1:
time: 71.1 us; the launch traced here: 70.8 us
  Pallas kernels  61.6 us (87%)
  local copies, waits for them, and re-layouts  8.49 us (12%)
    pallas_call x1, Pallas kernels, per_device(): call(out_shape=(full, full, jax.ShapeDtypeStruct((CL, T, AT), f32)), in_s...  61.6 us
    unnamed x8, local copies, waits for them, and re-layouts  5.38 us
    another operation x2, local copies, waits for them, and re-layouts, per_device(): jnp.tile(r2.T, (1, 3 * A))  1.49 us

profile of v1, /device:TPU:0, one launch (start us, length us, event | category | flops | bytes accessed | tf_op | source)
XLA Modules:
  0.0 70.8 jit_solution(10268862503093758359)
XLA Ops:
  0.6 0.8 %fusion = f32[8,6]{0,1:T(8,128)S(1)} fusion(s32[]{:T(128)S(6)} %select_n.6, s32[]{:T(128)S(6)} %select_n.7, f32[128,256]{1,0:T(8,128)} %param.17), kind=kLoop, calls=%fused_computation.1 | loop fusion | bytes 131272 | tf_op jit(solution)/shard_map/transpose | solution.py:526
  1.4 0.1 copy.18
  1.5 0.1 pad.9.clone
  1.6 0.1 broadcast_in_dim.3
  1.7 0.7 reshape.13.rest_3_
  2.3 0.7 %tile.4 = f32[64,12,32]{0,2,1:T(8,128)S(1)} broadcast(f32[64,32]{0,1:T(8,128)} %bitcast.5), dimensions={0,2} | broadcast | bytes 106496 | tf_op jit(solution)/shard_map/tile | solution.py:536
  3.1 0.8 %copy.17.rest_2_ = f32[64,384]{1,0:T(8,128)} copy(f32[64,384]{0,1:T(8,128)S(1)} %bitcast.4) | data formatting | bytes 196608 | tf_op jit(solution)/shard_map/tile | solution.py:536
  3.8 61.6 %shard_map.130 = (f32[8,64,1024]{2,1,0:T(8,128)}, f32[8,64,1024]{2,1,0:T(8,128)}, f32[8,32,128]{2,1,0:T(8,128)}) custom-call(f32[4]{0:T(128)} %shift_ref.1, f32[8,64,1024]{2,1,0:T(8,128)} %volt_hbm.1, f32[8,64,1024]{2,1,0:T(8,128)} %start_hbm.1, f32[8,64,1024]{2,1,0:T(8,128)} %gen_hbm.1, f32[8,64,1024]{2,1,0:T(8,128)} %ann_hbm.1, s32[8,64,1024]{2,1,0:T(8,128)} %grain_hbm.1, ...), custom_call_target="tpu_custom_call" | custom-call | flops 104857600 | bytes 14680064 | tf_op jit(solution)/shard_map/pallas_call | solution.py:528
  65.5 0.0 copy-start.1
  65.5 0.0 copy-start
  65.5 3.3 %copy.22 = f32[8,64,1024]{2,1,0:T(8,128)} copy(f32[8,64,1024]{2,1,0:T(8,128)} %get-tuple-element.12) | data formatting | bytes 4194304
  68.8 0.0 copy-done.1
  68.8 0.7 copy.23
  69.5 0.0 copy-done
  69.5 1.3 %copy.24 = f32[8,64,1024]{2,1,0:T(8,128)} copy(f32[8,64,1024]{2,1,0:T(8,128)S(1)} %copy-done) | data formatting | bytes 4194304
Async XLA Ops:
  65.5 3.3 %copy-start.1 = (f32[8,32,128]{2,1,0:T(8,128)S(1)}, f32[8,32,128]{2,1,0:T(8,128)}, u32[]{:S(2)}) copy-start(f32[8,32,128]{2,1,0:T(8,128)} %get-tuple-element.13) | copy-start | bytes 393220
  65.5 4.0 %copy-start = (f32[8,64,1024]{2,1,0:T(8,128)S(1)}, f32[8,64,1024]{2,1,0:T(8,128)}, u32[]{:S(2)}) copy-start(f32[8,64,1024]{2,1,0:T(8,128)} %get-tuple-element.14) | copy-start | bytes 6291460

commit v2 on v1

--- a/solution.py
+++ b/solution.py
@@ -38,13 +38,12 @@
     extra_in, rest = rest[:count], rest[count:]
     count = 3 if yblocks == 1 else 2
     (dens_hbm, *extra_out), rest = rest[:count], rest[count:]
-    (E, N0, N1, N2, GEN, ANN, GR, RD, BX, MX, BY, MY, BZ, MZ, B0, U0, HEAT, R3,
+    (E, N0, N1, N2, GEN, ANN, GR, RD, BX, MX, BY, MY, BZ, MZ, U0, HEAT, R3,
      in_sem, out_sem, send_sem, recv_sem, *extra) = rest
     X, Y, Z = GEN.shape
     me = lax.axis_index("slab")
     gy = lax.axis_index("gy")
     rows = slice(PAD, PAD + Y)
-    chunks = range(0, Y, 8)
 
     loads = {}
 
@@ -79,6 +78,8 @@
         def _():
             buf[X + 1, rows, :] = zero_layer
 
+    barrier = pltpu.get_barrier_semaphore()
+
     def others(body):
         def step(i, carry):
             body(lax.rem(me + i, slabs))
@@ -86,14 +87,35 @@
         lax.fori_loop(1, slabs, step, 0)
 
     if yblocks == 1:
-        warm_ref, cool_ref, r2_tile, wx_rows = extra_in
-        fine_hbm, thermal_ref = extra_out
-        P, TRC, TR, SRC, W, SL, SR, GOTL, GOTR, OWN, RCV, all_send, all_recv = extra
+        warm_ref, cool_ref, r1_ref, r2_ref = extra_in
+        spread_ref, RCV = extra_out
+        P, TRC, TR, SRC, W, SL, SR, GOTL, GOTR, OWN, LAND, all_send, all_recv = extra
         CL, T, AT = warm_ref.shape
         A = AT // slabs
         AW = A * T
         group = 128 // T
+        others_rows = CL * (slabs - 1)
         low, mid, high = slice(0, AW), slice(AW, 2 * AW), slice(2 * AW, 3 * AW)
+
+        @pl.when(me == 0)
+        def _():
+            GOTL[...] = jnp.zeros_like(GOTL)
+            TRC[:, :, low] = jnp.zeros((2, CL * slabs, AW), jnp.float32)
+
+        @pl.when(me == slabs - 1)
+        def _():
+            GOTR[...] = jnp.zeros_like(GOTR)
+            TRC[:, :, high] = jnp.zeros((2, CL * slabs, AW), jnp.float32)
+        others(lambda d: pl.semaphore_signal(barrier, inc=1, device_id=(d, gy), device_id_type=MESH))
+
+        place = lax.broadcasted_iota
+        pick_x = place(jnp.int32, (X, slabs * X), 1) == me * X + place(jnp.int32, (X, slabs * X), 0)
+        pick_a = place(jnp.int32, (AT, 3 * AW), 0) == me * A - A + place(jnp.int32, (AT, 3 * AW), 1) // T
+        wx_rows = product(pick_x.astype(jnp.float32), r1_ref[...], ((1,), (1,)))
+        wx_rows = product(wx_rows, pick_a.astype(jnp.float32))
+        r2_tile = jnp.concatenate([r2_ref[...].T] * (3 * A), axis=1)
+        for x in range(X):
+            W[x * Y:(x + 1) * Y, :] = r2_tile * wx_rows[x:x + 1, :]
 
         for k in range(2):
             for c0 in range(0, CL, group):
@@ -109,36 +131,24 @@
             return pl.ds(pl.multiple_of(d * CL, CL), CL)
 
         TRC[:, slab_rows(me), mid] = P[:, slab_rows(me), :]
+        pl.semaphore_wait(barrier, slabs - 1)
+
+    else:
+        SEND, HZ, GOTL, GOTR = extra
+        wx_ref, ky_ref = extra_in
 
         @pl.when(me == 0)
         def _():
             GOTL[...] = jnp.zeros_like(GOTL)
-            TRC[:, :, low] = jnp.zeros((2, CL * slabs, AW), jnp.float32)
 
         @pl.when(me == slabs - 1)
         def _():
             GOTR[...] = jnp.zeros_like(GOTR)
-            TRC[:, :, high] = jnp.zeros((2, CL * slabs, AW), jnp.float32)
-    else:
-        SEND, HZ, GOTL, GOTR = extra
-        wx_ref, ky_ref = extra_in
-
-        @pl.when(me == 0)
-        def _():
-            GOTL[...] = jnp.zeros_like(GOTL)
-
-        @pl.when(me == slabs - 1)
-        def _():
-            GOTR[...] = jnp.zeros_like(GOTR)
 
     x_sides = [(me > 0, (me - 1, gy)), (me < slabs - 1, (me + 1, gy))]
     y_sides = [] if yblocks == 1 else [(gy > 0, (me, gy - 1)), (gy < yblocks - 1, (me, gy + 1))]
 
-    barrier = pltpu.get_barrier_semaphore()
-    if yblocks == 1:
-        others(lambda d: pl.semaphore_signal(barrier, inc=1, device_id=(d, gy), device_id_type=MESH))
-        pl.semaphore_wait(barrier, slabs - 1)
-    else:
+    if yblocks > 1:
         for has, device in x_sides + y_sides:
             @pl.when(has)
             def _():
@@ -188,26 +198,48 @@
         start(copies)
         finish(copies)
 
-    def over_layers(first, last, body):
-        def step(x, carry):
-            body(x)
+    def over_layers(count, layer_of, body, at=None, action=None):
+        def step(i, carry):
+            if at is not None:
+                pl.when(i == at)(action)
+            body(layer_of(i))
             return carry
-        lax.fori_loop(first, last, step, 0)
+        lax.fori_loop(0, count, step, 0)
+
+    def over_chunks(body, init=0):
+        lax.fori_loop(0, Y // 8, lambda k, carry: body(pl.multiple_of(k * 8, 8), carry), init, unroll=2)
+
+    def ends_first(i):
+        return jnp.where(i == 0, 0, jnp.where(i == 1, X - 1, i - 1))
+
+    def ends_last(i):
+        return jnp.where(i < X - 2, i + 1, jnp.where(i == X - 2, 0, X - 1))
+
+    row8 = lax.broadcasted_iota(jnp.int32, (8, Z), 0)
+
+    def up_y(v, following):
+        return pltpu.roll(jnp.where(row8 == 0, following, v), 7, 0)
+
+    def down_y(v, preceding):
+        return pltpu.roll(jnp.where(row8 == 7, preceding, v), 1, 0)
 
     shifts = [shift_ref[g] for g in range(GRAINS)]
 
     def effective(x):
-        for y in chunks:
-            grain = GR[x, y:y + 8, :]
+        def chunk(y, carry):
+            c, r = pl.ds(y, 8), pl.ds(y + PAD, 8)
+            grain = GR[x, c, :]
             shift = jnp.where(grain == 0, shifts[0], 0.0)
             for g in range(1, GRAINS):
                 shift = jnp.where(grain == g, shifts[g], shift)
-            E[x + 1, PAD + y:PAD + y + 8, :] = E[x + 1, PAD + y:PAD + y + 8, :] + shift
+            E[x + 1, r, :] = E[x + 1, r, :] + shift
+            return carry
+        over_chunks(chunk)
 
     for layer in (0, X - 1):
         loads[("v", layer)].wait()
         loads[("g", layer)].wait()
-        effective(layer)
+    over_layers(2, lambda i: i * (X - 1), effective)
     e_copies = x_copies(0, E)
     start(e_copies)
     for layer in (0, X - 1):
@@ -217,9 +249,12 @@
 
     def all_copy(k, src, dst, d, s):
         return pltpu.make_async_remote_copy(
-            src_ref=src, dst_ref=dst, send_sem=all_send.at[k, d], recv_sem=all_recv.at[k, s],
+            src_ref=src, dst_ref=dst, send_sem=all_send.at[k], recv_sem=all_recv.at[k],
             device_id=(d, gy), device_id_type=MESH,
         )
+
+    def wait_all(k, sem, ref):
+        pltpu.make_async_copy(ref, ref, sem.at[k]).wait()
 
     if yblocks == 1:
         def spread_copy(d, s):
@@ -228,7 +263,7 @@
         others(lambda d: spread_copy(d, me).start())
     loads["v"].wait()
     loads["g"].wait()
-    over_layers(1, X - 1, effective)
+    over_layers(X - 2, lambda i: i + 1, effective)
     loads["n"].wait()
     if y_sides:
         exchange_y(0, E)
@@ -248,50 +283,55 @@
         return pltpu.roll(v, 1, 1)
 
     def yz_faces(x):
-        u = E[x + 1, PAD:PAD + 8, :] - E[x + 1, PAD - 1:PAD + 7, :]
+        e = E[x + 1, 0:PAD, :]
+        u = up_y(e, E[x + 1, PAD:PAD + 8, :]) - e
         b = bernoulli(u)
-        BY[x, PAD - 1:PAD, :] = b[0:1]
-        MY[x, PAD - 1:PAD, :] = b[0:1] + u[0:1]
-        for y in chunks:
-            r = PAD + y
-            e = E[x + 1, r:r + 8, :]
-            uy = E[x + 1, r + 1:r + 9, :] - e
+        BY[x, 0:PAD, :] = b
+        MY[x, 0:PAD, :] = b + u
+
+        def chunk(y, below):
+            c, r = pl.ds(y, 8), pl.ds(y + PAD, 8)
+            e = E[x + 1, r, :]
+            uy = up_y(e, E[x + 1, pl.ds(y + PAD + 8, 8), :]) - e
             by = bernoulli(uy)
             my = by + uy
-            BY[x, r:r + 8, :] = by
-            MY[x, r:r + 8, :] = my
+            BY[x, r, :] = by
+            MY[x, r, :] = my
             uz = up_z(e) - e
             bz = bernoulli(uz)
             mz = jnp.where(last_lane, 0.0, bz + uz)
             bz = jnp.where(last_lane, 0.0, bz)
-            BZ[x, y:y + 8, :] = bz
-            MZ[x, y:y + 8, :] = mz
+            BZ[x, c, :] = bz
+            MZ[x, c, :] = mz
             e0 = jnp.where(lane0, e[:, head], e[:, tail])
             b0 = bernoulli(e0)
-            U0[x, y:y + 8, :] = 0.5 * e0 * b0
-            total = ANN[x, y:y + 8, :] + my + mz + down_z(bz) + BY[x, r - 1:r + 7, :]
-            RD[x, y:y + 8, :] = total
-            RD[x, y:y + 8, head] = total[:, head] + jnp.where(lane0, b0, 0.0)
-            RD[x, y:y + 8, tail] = total[:, tail] + jnp.where(lane1, b0, 0.0)
-
-    over_layers(0, X, yz_faces)
+            U0[x, c, :] = 0.5 * e0 * b0
+            total = ANN[x, c, :] + my + mz + down_z(bz) + down_y(by, below)
+            RD[x, c, :] = total
+            RD[x, c, head] = total[:, head] + jnp.where(lane0, b0, 0.0)
+            RD[x, c, tail] = total[:, tail] + jnp.where(lane1, b0, 0.0)
+            return by
+        over_chunks(chunk, b)
+
+    over_layers(X, lambda i: i, yz_faces)
 
     def x_face(f):
-        for y in chunks:
-            r = PAD + y
-            u = E[f + 1, r:r + 8, :] - E[f, r:r + 8, :]
+        def chunk(y, carry):
+            c, r = pl.ds(y, 8), pl.ds(y + PAD, 8)
+            u = E[f + 1, r, :] - E[f, r, :]
             b = bernoulli(u)
-            BX[f, y:y + 8, :] = b
-            MX[f, y:y + 8, :] = b + u
-
-    over_layers(1, X, x_face)
-    finish(e_copies)
-    x_face(0)
-    x_face(X)
+            BX[f, c, :] = b
+            MX[f, c, :] = b + u
+            return carry
+        over_chunks(chunk)
+
+    over_layers(
+        X + 1, lambda i: jnp.where(i < X - 1, i + 1, (i - (X - 1)) * X), x_face, X - 1, lambda: finish(e_copies)
+    )
     loads["gen"].wait()
     finish(n_copies)
     if yblocks == 1:
-        others(lambda s: spread_copy(s, s).wait_recv())
+        wait_all(0, all_recv, TRC.at[:, pl.ds(0, others_rows), pl.ds(AW, AW)])
         block_copies = [
             (has, side_copy(5, d, device, TRC.at[:, :, pl.ds(AW, AW)], TRC.at[:, :, pl.ds(2 * AW if d == 0 else 0, AW)]))
             for d, (has, device) in enumerate(x_sides)
@@ -299,37 +339,35 @@
 
     def sweep(src, dst, first):
         def layer(x):
-            for y in chunks:
-                r = PAD + y
-                c = slice(y, y + 8)
-                n = src[x + 1, r:r + 8, :]
-                total = GEN[x, c, :] + BX[x + 1, c, :] * src[x + 2, r:r + 8, :] + MX[x, c, :] * src[x, r:r + 8, :]
-                total = total + BY[x, r:r + 8, :] * src[x + 1, r + 1:r + 9, :]
-                total = total + MY[x, r - 1:r + 7, :] * src[x + 1, r - 1:r + 7, :]
+            def chunk(y, below):
+                c, r = pl.ds(y, 8), pl.ds(y + PAD, 8)
+                n = src[x + 1, r, :]
+                total = GEN[x, c, :] + BX[x + 1, c, :] * src[x + 2, r, :] + MX[x, c, :] * src[x, r, :]
+                total = total + BY[x, r, :] * up_y(n, src[x + 1, pl.ds(y + PAD + 8, 8), :])
+                product_y = MY[x, r, :] * n
+                total = total + down_y(product_y, below)
                 total = total + BZ[x, c, :] * up_z(n) + down_z(MZ[x, c, :] * n)
                 if first:
                     rd = inverse(RD[x, c, :] + MX[x + 1, c, :] + BX[x, c, :])
                     RD[x, c, :] = rd
                 else:
                     rd = RD[x, c, :]
-                dst[x + 1, r:r + 8, :] = total * rd
+                dst[x + 1, r, :] = total * rd
+                return product_y
+            over_chunks(chunk, MY[x, 0:PAD, :] * src[x + 1, 0:PAD, :])
         return layer
 
-    first = sweep(N0, N1, True)
-    over_layers(0, 1, first)
-    over_layers(X - 1, X, first)
     one_copies = x_copies(2, N1)
-    start(one_copies)
-    if yblocks == 1:
-        start(block_copies)
-    over_layers(1, X - 1, first)
+
+    def send_one():
+        start(one_copies)
+        if yblocks == 1:
+            start(block_copies)
+
+    over_layers(X, ends_first, sweep(N0, N1, True), 2, send_one)
     if y_sides:
         exchange_y(2, N1)
-    second = sweep(N1, N2, False)
-    over_layers(1, X - 1, second)
-    finish(one_copies)
-    over_layers(0, 1, second)
-    over_layers(X - 1, X, second)
+    over_layers(X, ends_last, sweep(N1, N2, False), X - 2, lambda: finish(one_copies))
     two_copies = x_copies(3, N2)
     start(two_copies)
     out = pltpu.make_async_copy(N2.at[pl.ds(1, X), pl.ds(PAD, Y)], dens_hbm, out_sem)
@@ -338,8 +376,6 @@
         exchange_y(3, N2)
 
     def solve_and_prolong():
-        for x in range(X):
-            W[x * Y:(x + 1) * Y, :] = r2_tile[...] * wx_rows[x:x + 1, :]
         along_z = product(R3[...], HEAT[...].reshape(X * Y, Z), ((1,), (1,)))
         SL[...] = product(along_z, W[:, AW - T:2 * AW - T])
         SR[...] = product(along_z, W[:, AW + T:2 * AW + T])
@@ -373,62 +409,44 @@
         OWN[...] = TRC[0, :, mid]
 
         def back_copy(d, s):
-            return all_copy(1, OWN.at[slab_rows(d)], RCV.at[slab_rows(s)], d, s)
+            return all_copy(1, OWN.at[slab_rows(d)], LAND.at[slab_rows(s)], d, s)
 
         others(lambda d: back_copy(d, me).start())
-        RCV[slab_rows(me), :] = OWN[slab_rows(me), :]
-        spread = 16.0 * product(W[:, AW - T:2 * AW + T], TRC[0, :, AW - T:2 * AW + T], ((1,), (1,)))
-        writes = []
-        for x in range(0, X, 2):
-            HEAT[x:x + 2] = product(spread[x * Y:(x + 2) * Y], R3[...]).reshape(2, Y, Z)
-            writes.append(pltpu.make_async_copy(
-                HEAT.at[pl.ds(x, 2)], fine_hbm.at[pl.ds(x, 2)], in_sem.at[len(loads) + len(writes)]
-            ))
-            writes[-1].start()
-        others(lambda s: back_copy(s, s).wait_recv())
-        for c0 in range(0, CL, group):
-            cols = [RCV[pl.ds(c0 + c, slabs, stride=CL), :] for c in range(group)]
-            for j in range(A):
-                TR[pl.ds(j, slabs, stride=A), :] = jnp.concatenate(
-                    [v[:, j * T:(j + 1) * T] for v in cols], axis=1
-                )
-            thermal_ref[c0:c0 + group] = TR[...].T.reshape(group, T, AT)
-        others(lambda d: back_copy(d, me).wait_send())
-        for write in writes:
-            write.wait()
+        LAND[slab_rows(me), :] = OWN[slab_rows(me), :]
+        spread_ref[...] = 16.0 * product(W[:, AW - T:2 * AW + T], TRC[0, :, AW - T:2 * AW + T], ((1,), (1,)))
+        wait_all(1, all_recv, LAND.at[pl.ds(0, others_rows)])
+        RCV[...] = LAND[...]
+        wait_all(1, all_send, OWN.at[pl.ds(0, others_rows)])
 
     def heat(x):
-        for y in chunks:
-            r = PAD + y
-            c = slice(y, y + 8)
-            n = N2[x + 1, r:r + 8, :]
-
-            def term(b, m, low, high):
-                return (m - b) * (b * high - m * low)
-
-            total = term(BX[x + 1, c, :], MX[x + 1, c, :], n, N2[x + 2, r:r + 8, :])
-            total = total + term(BX[x, c, :], MX[x, c, :], N2[x, r:r + 8, :], n)
-            total = total + term(BY[x, r:r + 8, :], MY[x, r:r + 8, :], n, N2[x + 1, r + 1:r + 9, :])
-            total = total + term(
-                BY[x, r - 1:r + 7, :], MY[x, r - 1:r + 7, :], N2[x + 1, r - 1:r + 7, :], n
-            )
+        def term(b, m, low, high):
+            return (m - b) * (b * high - m * low)
+
+        def y_term(r, n, following):
+            return term(BY[x, r, :], MY[x, r, :], n, up_y(n, following))
+
+        def chunk(y, below):
+            c, r = pl.ds(y, 8), pl.ds(y + PAD, 8)
+            n = N2[x + 1, r, :]
+            total = term(BX[x + 1, c, :], MX[x + 1, c, :], n, N2[x + 2, r, :])
+            total = total + term(BX[x, c, :], MX[x, c, :], N2[x, r, :], n)
+            fy = y_term(r, n, N2[x + 1, pl.ds(y + PAD + 8, 8), :])
+            total = total + fy + down_y(fy, below)
             fz = term(BZ[x, c, :], MZ[x, c, :], n, up_z(n))
-            total = total + fz + down_z(fz)
-            total = 0.5 * total
+            total = 0.5 * (total + fz + down_z(fz))
             HEAT[x, c, :] = total
             u0 = U0[x, c, :]
             HEAT[x, c, head] = total[:, head] + jnp.where(lane0, u0 * n[:, head], 0.0)
             HEAT[x, c, tail] = total[:, tail] + jnp.where(lane1, u0 * n[:, tail], 0.0)
-
-    over_layers(1, X - 1, heat)
-    finish(two_copies)
-    over_layers(0, 1, heat)
-    over_layers(X - 1, X, heat)
+            return fy
+        over_chunks(chunk, y_term(slice(0, PAD), N2[x + 1, 0:PAD, :], N2[x + 1, PAD:PAD + 8, :]))
+
+    over_layers(X, ends_last, heat, X - 2, lambda: finish(two_copies))
 
     loads["r3"].wait()
     if yblocks == 1:
         finish(block_copies)
-        others(lambda d: spread_copy(d, me).wait_send())
+        wait_all(0, all_send, P.at[:, pl.ds(0, others_rows)])
         solve_and_prolong()
         out.wait()
         return
@@ -464,6 +482,24 @@
     out.wait()
 
 
+def finish_kernel(spread_ref, r3_ref, dens_ref, got_ref, fine_ref, dens_out, thermal_ref, tr):
+    CL, T, AT = thermal_ref.shape
+    A = got_ref.shape[1] // T
+    slabs, group = AT // A, 128 // T
+    dens_out[...] = dens_ref[...]
+    fine_ref[...] = product(spread_ref[...], r3_ref[...]).reshape(fine_ref.shape)
+
+    @pl.when(pl.program_id(0) == 0)
+    def _():
+        for c0 in range(0, CL, group):
+            cols = [got_ref[pl.ds(c0 + c, slabs, stride=CL), :] for c in range(group)]
+            for j in range(A):
+                tr[pl.ds(j, slabs, stride=A), :] = jnp.concatenate(
+                    [v[:, j * T:(j + 1) * T] for v in cols], axis=1
+                )
+            thermal_ref[c0:c0 + group] = tr[...].T.reshape(group, T, AT)
+
+
 def prolong_kernel(wx_ref, t_ref, ky_ref, r3_ref, out_ref, spread):
     X = wx_ref.shape[1]
     A = X // 2
@@ -506,7 +542,7 @@
     cells = X * Y * Z
     scratch = [
         padded, padded, padded, padded, block, block, pltpu.VMEM((X, Y, Z), jnp.int32), block,
-        xface, xface, yface, yface, block, block, edge, edge, block, pltpu.VMEM((C, Z), f32),
+        xface, xface, yface, yface, block, block, edge, block, pltpu.VMEM((C, Z), f32),
         pltpu.SemaphoreType.DMA((20,)), pltpu.SemaphoreType.DMA,
         pltpu.SemaphoreType.DMA((6, 4)), pltpu.SemaphoreType.DMA((6, 4)),
     ]
@@ -523,17 +559,36 @@
 
     if yblocks == 1:
         AW = A * T
-        wx_rows = jnp.pad(wx.T, ((0, 0), (A - 1, A - 1)))
-        wx_rows = jnp.repeat(wx_rows, T, axis=1)
-        density, fine, thermal_out = call(
-            out_shape=(full, full, jax.ShapeDtypeStruct((CL, T, AT), f32)),
+        density, spread, got = call(
+            out_shape=(
+                full, jax.ShapeDtypeStruct((X * Y, C), f32), jax.ShapeDtypeStruct((C, AW), f32)
+            ),
             in_specs=[smem] + [anyspace] * 6 + [vmem] * 4,
-            out_specs=(anyspace, anyspace, vmem),
+            out_specs=(anyspace, vmem, vmem),
             scratch_shapes=scratch + [
                 pltpu.VMEM((2, C, AW), f32), pltpu.VMEM((2, C, 3 * AW), f32), pltpu.VMEM((AT, 128), f32),
                 pltpu.VMEM((C, 3 * AW), f32), pltpu.VMEM((X * Y, 3 * AW), f32),
-            ] + [pltpu.VMEM((C, AW), f32)] * 6 + [pltpu.SemaphoreType.DMA((2, slabs))] * 2,
-        )(*operands, warming, cooling, jnp.tile(r2.T, (1, 3 * A)), wx_rows)
+            ] + [pltpu.VMEM((C, AW), f32)] * 6 + [pltpu.SemaphoreType.DMA((2,))] * 2,
+        )(*operands, warming, cooling, r1, r2)
+        steps = X // 2
+        layers = pl.BlockSpec((X // steps, Y, Z), lambda i: (i, 0, 0))
+        fine, density, thermal_out = pl.pallas_call(
+            finish_kernel,
+            grid=(steps,),
+            out_shape=(full, full, jax.ShapeDtypeStruct((CL, T, AT), f32)),
+            in_specs=[
+                pl.BlockSpec((X * Y // steps, C), lambda i: (i, 0)),
+                pl.BlockSpec((C, Z), lambda i: (0, 0)),
+                layers,
+                pl.BlockSpec((C, AW), lambda i: (0, 0)),
+            ],
+            out_specs=(layers, layers, pl.BlockSpec((CL, T, AT), lambda i: (0, 0, 0))),
+            scratch_shapes=[pltpu.VMEM((AT, 128), f32)],
+            compiler_params=pltpu.CompilerParams(vmem_limit_bytes=24 * MIB),
+            cost_estimate=pl.CostEstimate(
+                flops=12 * X * Y * C * Z, bytes_accessed=4 * (3 * cells + C * Z), transcendentals=0
+            ),
+        )(spread, r3, density, got)
         return density, thermal_out, fine
 
     eye = jnp.eye(X, dtype=f32)

time: 71.1 us -> 68.8 us (0.968)
  local copies, waits for them, and re-layouts: 8.49 us -> 3.53 us
  Pallas kernels: 61.6 us -> 64.4 us
    pallas_call x1 -> x2, Pallas kernels: 61.6 us -> 64.4 us  [the longest x1 60.2 us: per_device(): call(out_shape=(full, jax.ShapeDtypeStruct((X * Y, C), f32), jax.ShapeDty...]
    unnamed x8, local copies, waits for them, and re-layouts: 5.38 us -> 3.53 us
    another operation x2 -> x0, local copies, waits for them, and re-layouts: 1.49 us -> none  [per_device(): jnp.tile(r2.T, (1, 3 * A))]
    transpose x1 -> x0, local copies, waits for them, and re-layouts: 0.78 us -> none  [per_device(): wx_rows = jnp.pad(wx.T, ((0, 0), (A - 1, A - 1)))]
where the time goes in v2:
time: 68.8 us; the launch traced here: 68.6 us
  Pallas kernels  64.4 us (94%)
  local copies, waits for them, and re-layouts  3.53 us (5%)
    pallas_call x1, Pallas kernels, per_device(): call(out_shape=(full, jax.ShapeDtypeStruct((X * Y, C), f32), jax.ShapeDty...  60.2 us
    pallas_call x1, Pallas kernels, per_device(): pl.pallas_call(finish_kernel, grid=(steps,), out_shape=(full, full, jax.S...  4.25 us
    unnamed x8, local copies, waits for them, and re-layouts  3.53 us

profile of v2, /device:TPU:0, one launch (start us, length us, event | category | flops | bytes accessed | tf_op | source)
XLA Modules:
  0.0 68.6 jit_solution(3119741292110002406)
XLA Ops:
  0.6 0.0 copy-start
  0.6 60.2 %shard_map.130 = (f32[8,64,1024]{2,1,0:T(8,128)}, f32[512,256]{1,0:T(8,128)}, f32[256,128]{1,0:T(8,128)}) custom-call(f32[4]{0:T(128)} %shift_ref.1, f32[8,64,1024]{2,1,0:T(8,128)} %volt_hbm.1, f32[8,64,1024]{2,1,0:T(8,128)} %start_hbm.1, f32[8,64,1024]{2,1,0:T(8,128)} %gen_hbm.1, f32[8,64,1024]{2,1,0:T(8,128)} %ann_hbm.1, s32[8,64,1024]{2,1,0:T(8,128)} %grain_hbm.1, ...), custom_call_target="tpu_custom_call" | custom-call | flops 104857600 | bytes 14680064 | tf_op jit(solution)/shard_map/pallas_call | solution.py:562
  60.8 0.0 copy-done
  60.8 0.0 copy-start.1
  60.8 1.6 %copy-done.1 = f32[8,64,1024]{2,1,0:T(8,128)S(1)} copy-done((f32[8,64,1024]{2,1,0:T(8,128)S(1)}, f32[8,64,1024]{2,1,0:T(8,128)}, u32[]{:S(2)}) %copy-start.1) | copy-done | bytes 2097176
  62.4 0.0 copy-start.2
  62.4 1.0 %copy-done.2 = f32[512,256]{1,0:T(8,128)S(1)} copy-done((f32[512,256]{1,0:T(8,128)S(1)}, f32[512,256]{1,0:T(8,128)}, u32[]{:S(2)}) %copy-start.2) | copy-done | bytes 524312
  63.5 0.0 copy-start.3
  63.5 0.9 %copy-done.3 = f32[256,128]{1,0:T(8,128)S(1)} copy-done((f32[256,128]{1,0:T(8,128)S(1)}, f32[256,128]{1,0:T(8,128)}, u32[]{:S(2)}) %copy-start.3) | copy-done | bytes 131096
  64.4 4.3 %shard_map.131 = (f32[8,64,1024]{2,1,0:T(8,128)}, f32[8,64,1024]{2,1,0:T(8,128)}, f32[8,32,128]{2,1,0:T(8,128)}) custom-call(f32[512,256]{1,0:T(8,128)S(1)} %copy-done.2, f32[256,1024]{1,0:T(8,128)S(1)} %copy-done, f32[8,64,1024]{2,1,0:T(8,128)S(1)} %copy-done.1, f32[256,128]{1,0:T(8,128)S(1)} %copy-done.3), custom_call_target="tpu_custom_call" | custom-call | flops 1610612736 | bytes 7340032 | tf_op jit(solution)/shard_map/pallas_call | solution.py:575
Async XLA Ops:
  0.6 60.2 %copy-start = (f32[256,1024]{1,0:T(8,128)S(1)}, f32[256,1024]{1,0:T(8,128)}, u32[]{:S(2)}) copy-start(f32[256,1024]{1,0:T(8,128)} %r3_ref.1) | copy-start | bytes 3145732
  60.8 1.6 %copy-start.1 = (f32[8,64,1024]{2,1,0:T(8,128)S(1)}, f32[8,64,1024]{2,1,0:T(8,128)}, u32[]{:S(2)}) copy-start(f32[8,64,1024]{2,1,0:T(8,128)} %get-tuple-element.10.dens_ref) | copy-start | bytes 6291460
  62.4 1.0 %copy-start.2 = (f32[512,256]{1,0:T(8,128)S(1)}, f32[512,256]{1,0:T(8,128)}, u32[]{:S(2)}) copy-start(f32[512,256]{1,0:T(8,128)} %get-tuple-element.9.spread_ref) | copy-start | bytes 1572868
  63.5 0.9 %copy-start.3 = (f32[256,128]{1,0:T(8,128)S(1)}, f32[256,128]{1,0:T(8,128)}, u32[]{:S(2)}) copy-start(f32[256,128]{1,0:T(8,128)} %get-tuple-element.11.got_ref) | copy-start | bytes 393220

commit v3 on v2

--- a/solution.py
+++ b/solution.py
@@ -28,6 +28,18 @@
 
 def product(a, b, dims=((1,), (0,))):
     return lax.dot_general(a, b, (dims, ((), ())), precision=HIGHEST, preferred_element_type=jnp.float32)
+
+
+def halves(v):
+    high = v.astype(jnp.bfloat16)
+    return high, (v - high.astype(jnp.float32)).astype(jnp.bfloat16)
+
+
+def split_product(a, b, dims=((1,), (0,))):
+    def dot(p, q):
+        return lax.dot_general(p, q, (dims, ((), ())), preferred_element_type=jnp.float32)
+
+    return dot(a[0], b[0]) + (dot(a[0], b[1]) + dot(a[1], b[0]))
 
 
 def device_kernel(
@@ -80,6 +92,9 @@
 
     barrier = pltpu.get_barrier_semaphore()
 
+    def slot_of(x):
+        return (x + X - 2) if x == 0 else (x if x == X - 1 else x - 1)
+
     def others(body):
         def step(i, carry):
             body(lax.rem(me + i, slabs))
@@ -89,7 +104,7 @@
     if yblocks == 1:
         warm_ref, cool_ref, r1_ref, r2_ref = extra_in
         spread_ref, RCV = extra_out
-        P, TRC, TR, SRC, W, SL, SR, GOTL, GOTR, OWN, LAND, all_send, all_recv = extra
+        P, TRC, TR, SRC, WR, WP, SL, SR, GOTL, GOTR, OWN, LAND, all_send, all_recv = extra
         CL, T, AT = warm_ref.shape
         A = AT // slabs
         AW = A * T
@@ -115,7 +130,13 @@
         wx_rows = product(wx_rows, pick_a.astype(jnp.float32))
         r2_tile = jnp.concatenate([r2_ref[...].T] * (3 * A), axis=1)
         for x in range(X):
-            W[x * Y:(x + 1) * Y, :] = r2_tile * wx_rows[x:x + 1, :]
+            rows_x = slice(slot_of(x) * Y, slot_of(x) * Y + Y)
+            w = r2_tile * wx_rows[x:x + 1, :]
+            w_left, w_right = w[:, AW - T:2 * AW - T], w[:, AW + T:2 * AW + T]
+            for k, half in enumerate(halves(jnp.concatenate([w_left, w_right], axis=1))):
+                WR[k, rows_x, :] = half
+            for k, half in enumerate(halves(w[:, AW - T:2 * AW + T])):
+                WP[k, rows_x, :] = half
 
         for k in range(2):
             for c0 in range(0, CL, group):
@@ -375,10 +396,11 @@
     if y_sides:
         exchange_y(3, N2)
 
-    def solve_and_prolong():
-        along_z = product(R3[...], HEAT[...].reshape(X * Y, Z), ((1,), (1,)))
-        SL[...] = product(along_z, W[:, AW - T:2 * AW - T])
-        SR[...] = product(along_z, W[:, AW + T:2 * AW + T])
+    def solve_and_prolong(inner_z, ends_z):
+        share = split_product(halves(inner_z), (WR[0, :inner_rows], WR[1, :inner_rows]))
+        share = share + split_product(halves(ends_z), (WR[0, inner_rows:], WR[1, inner_rows:]))
+        SL[...] = share[:, :AW]
+        SR[...] = share[:, AW:]
         copies = [
             (has, side_copy(4, d, device, SL if d == 0 else SR, GOTR if d == 0 else GOTL))
             for d, (has, device) in enumerate(x_sides)
@@ -413,12 +435,16 @@
 
         others(lambda d: back_copy(d, me).start())
         LAND[slab_rows(me), :] = OWN[slab_rows(me), :]
-        spread_ref[...] = 16.0 * product(W[:, AW - T:2 * AW + T], TRC[0, :, AW - T:2 * AW + T], ((1,), (1,)))
+        spread = 16.0 * split_product((WP[0], WP[1]), halves(TRC[0, :, AW - T:2 * AW + T]), ((1,), (1,)))
+        for x in range(X):
+            spread_ref[x * Y:(x + 1) * Y, :] = spread[slot_of(x) * Y:slot_of(x) * Y + Y]
         wait_all(1, all_recv, LAND.at[pl.ds(0, others_rows)])
         RCV[...] = LAND[...]
         wait_all(1, all_send, OWN.at[pl.ds(0, others_rows)])
 
     def heat(x):
+        slot = jnp.where(x == 0, X - 2, jnp.where(x == X - 1, X - 1, x - 1)) if yblocks == 1 else x
+
         def term(b, m, low, high):
             return (m - b) * (b * high - m * low)
 
@@ -434,22 +460,32 @@
             total = total + fy + down_y(fy, below)
             fz = term(BZ[x, c, :], MZ[x, c, :], n, up_z(n))
             total = 0.5 * (total + fz + down_z(fz))
-            HEAT[x, c, :] = total
+            HEAT[slot, c, :] = total
             u0 = U0[x, c, :]
-            HEAT[x, c, head] = total[:, head] + jnp.where(lane0, u0 * n[:, head], 0.0)
-            HEAT[x, c, tail] = total[:, tail] + jnp.where(lane1, u0 * n[:, tail], 0.0)
+            HEAT[slot, c, head] = total[:, head] + jnp.where(lane0, u0 * n[:, head], 0.0)
+            HEAT[slot, c, tail] = total[:, tail] + jnp.where(lane1, u0 * n[:, tail], 0.0)
             return fy
         over_chunks(chunk, y_term(slice(0, PAD), N2[x + 1, 0:PAD, :], N2[x + 1, PAD:PAD + 8, :]))
 
-    over_layers(X, ends_last, heat, X - 2, lambda: finish(two_copies))
-
-    loads["r3"].wait()
+    inner_rows = (X - 2) * Y
     if yblocks == 1:
+        over_layers(X - 2, lambda i: i + 1, heat)
+        loads["r3"].wait()
+        r3 = halves(R3[...])
+        flat = halves(HEAT[0:X - 2].reshape(inner_rows, Z))
+        inner_z = split_product(r3, flat, ((1,), (1,)))
+        finish(two_copies)
+        over_layers(2, lambda i: i * (X - 1), heat)
+        flat = halves(HEAT[X - 2:].reshape(2 * Y, Z))
+        ends_z = split_product(halves(R3[...]), flat, ((1,), (1,)))
         finish(block_copies)
         wait_all(0, all_send, P.at[:, pl.ds(0, others_rows)])
-        solve_and_prolong()
+        solve_and_prolong(inner_z, ends_z)
         out.wait()
         return
+
+    over_layers(X, ends_last, heat, X - 2, lambda: finish(two_copies))
+    loads["r3"].wait()
     HZ[...] = product(HEAT[...].reshape(X * Y, Z), R3[...], ((1,), (1,))).reshape(HZ.shape)
     A = X // 2
     parts = []
@@ -487,7 +523,7 @@
     A = got_ref.shape[1] // T
     slabs, group = AT // A, 128 // T
     dens_out[...] = dens_ref[...]
-    fine_ref[...] = product(spread_ref[...], r3_ref[...]).reshape(fine_ref.shape)
+    fine_ref[...] = split_product(halves(spread_ref[...]), halves(r3_ref[...])).reshape(fine_ref.shape)
 
     @pl.when(pl.program_id(0) == 0)
     def _():
@@ -567,7 +603,8 @@
             out_specs=(anyspace, vmem, vmem),
             scratch_shapes=scratch + [
                 pltpu.VMEM((2, C, AW), f32), pltpu.VMEM((2, C, 3 * AW), f32), pltpu.VMEM((AT, 128), f32),
-                pltpu.VMEM((C, 3 * AW), f32), pltpu.VMEM((X * Y, 3 * AW), f32),
+                pltpu.VMEM((C, 3 * AW), f32), pltpu.VMEM((2, X * Y, 2 * AW), jnp.bfloat16),
+                pltpu.VMEM((2, X * Y, AW + 2 * T), jnp.bfloat16),
             ] + [pltpu.VMEM((C, AW), f32)] * 6 + [pltpu.SemaphoreType.DMA((2,))] * 2,
         )(*operands, warming, cooling, r1, r2)
         steps = X // 2
@@ -584,7 +621,7 @@
             ],
             out_specs=(layers, layers, pl.BlockSpec((CL, T, AT), lambda i: (0, 0, 0))),
             scratch_shapes=[pltpu.VMEM((AT, 128), f32)],
-            compiler_params=pltpu.CompilerParams(vmem_limit_bytes=24 * MIB),
+            compiler_params=pltpu.CompilerParams(vmem_limit_bytes=58 * MIB),
             cost_estimate=pl.CostEstimate(
                 flops=12 * X * Y * C * Z, bytes_accessed=4 * (3 * cells + C * Z), transcendentals=0
             ),

time: 68.8 us -> 65.9 us (0.958)
  local copies, waits for them, and re-layouts: 3.53 us -> 0 us
    unnamed x8 -> x0, local copies, waits for them, and re-layouts: 3.53 us -> none
    pallas_call x1, Pallas kernels: 4.25 us -> 5.74 us  [per_device(): pl.pallas_call(finish_kernel, grid=(steps,), out_shape=(full, full, jax.S...]
    pallas_call x1, Pallas kernels: 60.2 us -> 59.3 us  [per_device(): call(out_shape=(full, jax.ShapeDtypeStruct((X * Y, C), f32), jax.ShapeDty...]
where the time goes in v3:
time: 65.9 us; the launch traced here: 65.6 us
  Pallas kernels  65 us (99%)
    pallas_call x1, Pallas kernels, per_device(): call(out_shape=(full, jax.ShapeDtypeStruct((X * Y, C), f32), jax.ShapeDty...  59.3 us
    pallas_call x1, Pallas kernels, per_device(): pl.pallas_call(finish_kernel, grid=(steps,), out_shape=(full, full, jax.S...  5.74 us

profile of v3, /device:TPU:0, one launch (start us, length us, event | category | flops | bytes accessed | tf_op | source)
XLA Modules:
  0.0 65.6 jit_solution(5733392884352043766)
XLA Ops:
  0.6 59.3 %shard_map.130 = (f32[8,64,1024]{2,1,0:T(8,128)}, f32[512,256]{1,0:T(8,128)}, f32[256,128]{1,0:T(8,128)}) custom-call(f32[4]{0:T(128)} %shift_ref.1, f32[8,64,1024]{2,1,0:T(8,128)} %volt_hbm.1, f32[8,64,1024]{2,1,0:T(8,128)} %start_hbm.1, f32[8,64,1024]{2,1,0:T(8,128)} %gen_hbm.1, f32[8,64,1024]{2,1,0:T(8,128)} %ann_hbm.1, s32[8,64,1024]{2,1,0:T(8,128)} %grain_hbm.1, ...), custom_call_target="tpu_custom_call" | custom-call | flops 104857600 | bytes 14680064 | tf_op jit(solution)/shard_map/pallas_call | solution.py:598
  59.9 5.7 %shard_map.131 = (f32[8,64,1024]{2,1,0:T(8,128)}, f32[8,64,1024]{2,1,0:T(8,128)}, f32[8,32,128]{2,1,0:T(8,128)}) custom-call(f32[512,256]{1,0:T(8,128)} %get-tuple-element.9.spread_ref, f32[256,1024]{1,0:T(8,128)} %r3_ref.1, f32[8,64,1024]{2,1,0:T(8,128)} %get-tuple-element.10.dens_ref, f32[256,128]{1,0:T(8,128)} %get-tuple-element.11.got_ref), custom_call_target="tpu_custom_call" | custom-call | flops 1610612736 | bytes 7340032 | tf_op jit(solution)/shard_map/pallas_call | solution.py:612
